TPU v7x, 256 devices: a whole 4x4x8 slice. The times are simulated.
256 devices in a mesh: seq: 128 (over x, y, z_lo, core), head: 2 (over z_hi).
Axes of the slice: x: 4, y: 4, z: 8 (z_hi: 2, z_lo: 4; z = z_hi * 4 + z_lo), core: 2. Of those that a mesh axis runs over, the one named last changes fastest.
Arguments:
- queries: bfloat16 [32768, 3584], P('seq', 'head'), may hold values from -64 to 64, as said below
- keys: bfloat16 [32768, 512], P('seq', 'head'), may hold values from -4 to 4, as said below
- values: bfloat16 [32768, 512], P('seq', 'head'), may hold values from -6 to 6
- vert_blocks: int32 [4, 64], P('head'), may hold values from 0 to 511, as said below
- slash_offsets: int32 [4, 3], P('head'), may hold values from 0 to 4, as said below
Outputs:
- attended: bfloat16 [32768, 3584], P('seq', 'head')
Inputs may be any that keep to these rules, and one draw needn't show every extreme that they name: `vert_blocks`: for each KV head, 64 distinct key block indices in increasing order; the range of 4 blocks of one device holds at most one of them; block 0 and the last block of the prompt are always among them. `slash_offsets`: for each KV head, 3 distinct offsets; 0 and 4 are always among them. Real-valued queries. Real-valued keys.
All inputs are finite; a program needn't handle non-finite values.
Results may differ from a plain program's by a relative error of at most 0.0049.
Values may be sent and summed in bfloat16 or wider, within the bound.
No kernel may reach another device: no remote copies, remote signals or barrier semaphores. Data moves between devices by JAX's collectives and lax.ppermute only.
A program may use at most 64 MiB of HBM per device.

v0:
```python
import functools

import jax
import jax.numpy as jnp
import numpy as np
from jax import lax
from jax.experimental import pallas as pl
from jax.experimental.pallas import tpu as pltpu
from jax.sharding import PartitionSpec as P

HD = 128
GROUP = 7
BLK = 64
NV = 64
ROWS = 256
HALF = 32
COLS = GROUP * HD
DIMS = (4, 4, 4, 2)
X, Y, Z, CORE = 0, 1, 2, 3
SCALE = HD ** (-0.5) * 1.4426950408889634
LIMIT = 2.0**100
CHUNK = 256
UNROLL = 4
CAPACITY = 2 * NV * HALF + 2 * CHUNK
NT = (((1,), (1,)), ((), ()))
VMEM_LIMIT = 32 * 1024 * 1024

vmem = pl.BlockSpec(memory_space=pltpu.VMEM)
smem = pl.BlockSpec(memory_space=pltpu.SMEM)


def partner_route(axis, mask):
    ids = np.arange(128).reshape(DIMS)
    route = []
    for place in np.ndindex(*DIMS):
        other = list(place)
        other[axis] ^= mask
        route.append((int(ids[place]), int(ids[tuple(other)])))
    return route


def swap(block, axis, mask):
    return lax.ppermute(block, "seq", partner_route(axis, mask))


def cross(block):
    route = [(source, target ^ 1) for source, target in partner_route(Z, 1)]
    return lax.ppermute(block, "seq", route)


def coords():
    device = lax.axis_index("seq")
    return device, device >> 5, (device >> 3) & 3, (device >> 1) & 3, device & 1


def prep_kernel(vert_ref, keys_ref, values_ref, keep_ref, send_ref):
    device, _, _, _, core = coords()
    first = device * (ROWS // BLK)

    def find(index, found):
        out = []
        for head in range(2):
            rel = vert_ref[head, index] - first
            inside = (rel >= 0) & (rel < ROWS // BLK)
            out.append(jnp.where(inside, rel, found[head]))
        return tuple(out)

    found = lax.fori_loop(0, NV, find, (jnp.int32(0), jnp.int32(0)))
    for head in range(2):
        cols = slice(head * HD, (head + 1) * HD)
        start = pl.ds(pl.multiple_of(found[head] * BLK, BLK), BLK)

        def fill(out_ref, cols=cols, start=start):
            for which, src in enumerate((keys_ref, values_ref)):
                out_ref[which, :ROWS] = src[:, cols]
                out_ref[which, ROWS:] = src[start, cols]

        @pl.when(core == head)
        def _(fill=fill):
            fill(keep_ref)

        @pl.when(core != head)
        def _(fill=fill):
            fill(send_ref)


def prep(vert_blocks, keys, values):
    shape = jax.ShapeDtypeStruct((2, ROWS + BLK, HD), jnp.bfloat16)
    return pl.pallas_call(
        prep_kernel,
        out_shape=(shape, shape),
        in_specs=[smem, vmem, vmem],
        out_specs=(vmem, vmem),
        name="prep",
    )(vert_blocks, keys, values)


def cost(micros):
    return pl.CostEstimate(flops=int(micros * 1.15e9), bytes_accessed=4 << 20, transcendentals=0)


def plan_kernel(vert_ref, after_ref, plan_ref):
    device, x0, y0, z0, core = coords()
    chip = device >> 1
    base = chip * 8 - 4
    for source in range(8):
        plan_ref[source, 0] = 0
    for slot in range(12):
        plan_ref[8, slot] = 0
    plan_ref[8, 12] = 99
    plan_ref[8, 13] = 99

    def mark(index, unused):
        block = vert_ref[core, index]
        rel = block - base
        owner = block >> 2
        x, y = (owner >> 5) ^ x0, ((owner >> 3) & 3) ^ y0
        x, y = x ^ (x >> 1), y ^ (y >> 1)
        where_in = ((((owner >> 1) & 3) ^ z0) << 1) | (owner & 1)

        @pl.when(block < chip * 8)
        def _():
            for first, outer, inner in ((0, x, y), (1, y, x)):
                source = 2 * outer + first
                number = plan_ref[source, 0]
                plan_ref[source, 1 + number] = (inner << 3) | where_in
                plan_ref[source, 0] = number + 1

        @pl.when((rel >= 0) & (rel < 12))
        def _():
            plan_ref[8, rel] = 1

            @pl.when(rel >= 4)
            def _():
                plan_ref[8, 11 + (rel >> 2)] = rel

        return unused

    lax.fori_loop(0, NV, mark, 0)


def split_kernel(q_ref, after_ref, own_ref, foreign_ref):
    core = coords()[-1]

    @pl.when(core == 0)
    def _():
        own_ref[...] = q_ref[:, :COLS]
        foreign_ref[...] = q_ref[:, COLS:]

    @pl.when(core == 1)
    def _():
        own_ref[...] = q_ref[:, COLS:]
        foreign_ref[...] = q_ref[:, :COLS]


def split(queries, after):
    shape = jax.ShapeDtypeStruct((ROWS, COLS), jnp.bfloat16)
    return pl.pallas_call(
        split_kernel,
        out_shape=(shape, shape),
        in_specs=[vmem, pl.BlockSpec(memory_space=pl.ANY)],
        out_specs=(vmem, vmem),
        cost_estimate=cost(1.5),
        name="split",
    )(queries, after)


def make_plan(vert_blocks, after):
    return pl.pallas_call(
        plan_kernel,
        out_shape=jax.ShapeDtypeStruct((9, 128), jnp.int32),
        in_specs=[smem, pl.BlockSpec(memory_space=pl.ANY)],
        out_specs=smem,
        cost_estimate=cost(3),
        name="plan",
    )(vert_blocks, after)


def band_kernel(
    foreign, plan_ref, slash_ref, q_ref, keep_ref, recv_ref, prev_ref,
    acc_ref, max_ref, key_ref, value_ref,
):
    device, _, _, _, core = coords()
    base = (device >> 1) * 8 - 4
    middle = slash_ref[core, 0] + slash_ref[core, 1] + slash_ref[core, 2] - 4
    value_ref[:, HD:] = jnp.ones((3 * ROWS, HD), jnp.bfloat16)
    for src, place in ((prev_ref, 0), (keep_ref, 1 + core), (recv_ref, 2 - core)):
        rows = pl.ds(pl.multiple_of(place * ROWS, ROWS), ROWS)
        key_ref[rows, :] = src[0, :ROWS]
        value_ref[rows, :HD] = src[1, :ROWS]
    vert_first, vert_second = plan_ref[8, 12], plan_ref[8, 13]
    row = lax.broadcasted_iota(jnp.int32, (BLK, 6 * BLK), 0)
    col = lax.broadcasted_iota(jnp.int32, (BLK, 6 * BLK), 1)
    piece = col // BLK
    diagonal = (piece == 0) & (col <= row)
    chip_half = 1 - core if foreign else core
    for step in range(4):
        place = chip_half * 4 + (step + 4)
        spots = [place, place - middle, place - 4, vert_first, vert_second]
        on = [None]
        for spot in spots[1:3]:
            on.append((base + spot >= 0) & (plan_ref[8, spot] == 0))
        for spot in spots[3:]:
            on.append(spot < place)
        allowed = diagonal
        for number in range(1, 5):
            allowed = allowed | ((piece == number) & (jnp.where(on[number], 1, 0) == 1))
        safe = [jnp.where(spot < 12, spot, 0) for spot in spots] + [place]
        windows = [pl.ds(pl.multiple_of(spot * BLK, BLK), BLK) for spot in safe]
        keys_here = jnp.concatenate([key_ref[w, :] for w in windows], axis=0)
        values_here = jnp.concatenate([value_ref[w, :] for w in windows], axis=0)
        q_rows = slice(step * BLK, (step + 1) * BLK)
        queries = jnp.concatenate(
            [q_ref[q_rows, g * HD : (g + 1) * HD] for g in range(GROUP)], axis=0
        )
        scores = lax.dot_general(queries, keys_here, NT, preferred_element_type=jnp.float32)
        weights = []
        for g in range(GROUP):
            part = jnp.where(allowed, scores[g * BLK : (g + 1) * BLK] * SCALE, -1e30)
            largest = jnp.max(part, axis=1, keepdims=True)
            weights.append(jnp.exp2(part - largest).astype(jnp.bfloat16))
            max_ref[g, q_rows, :] = jnp.broadcast_to(largest, (BLK, HD))
        mixed = jnp.dot(
            jnp.concatenate(weights, axis=0), values_here, preferred_element_type=jnp.float32
        )
        for g in range(GROUP):
            acc_ref[g, q_rows, :] = mixed[g * BLK : (g + 1) * BLK]


STATE = (
    jax.ShapeDtypeStruct((GROUP, ROWS, 2 * HD), jnp.float32),
    jax.ShapeDtypeStruct((GROUP, ROWS, HD), jnp.float32),
)


def band(name, foreign, plan, slash_offsets, queries, keep, recv, prev):
    return pl.pallas_call(
        functools.partial(band_kernel, foreign),
        out_shape=STATE,
        in_specs=[smem, smem] + [vmem] * 4,
        out_specs=(vmem, vmem),
        scratch_shapes=[
            pltpu.VMEM((3 * ROWS, HD), jnp.bfloat16),
            pltpu.VMEM((3 * ROWS, 2 * HD), jnp.bfloat16),
        ],
        compiler_params=pltpu.CompilerParams(vmem_limit_bytes=VMEM_LIMIT),
        cost_estimate=cost(3),
        name=name,
    )(plan, slash_offsets, queries, keep, recv, prev)


def vertical_kernel(groups, begin, end, last, *refs):
    plan_ref, refs = refs[0], refs[1:]
    queries, refs = refs[:groups], refs[groups:]
    state, refs = refs[: 2 * groups], refs[2 * groups :]
    pieces, outs, scratch = refs[:end], refs[end:-5], refs[-5:]
    key_ref, value_ref, max_ref, score_ref, bad_ref = scratch
    if last:
        result_ref, acc_ref = outs
        accs = [acc_ref]
    else:
        accs = outs[::2]
    tiles = [(index, g) for index in range(groups) for g in range(GROUP)]
    ahead = 2 if len(tiles) % 2 == 0 else len(tiles)
    per_chunk = CHUNK // HALF
    counts = [plan_ref[source, 0] for source in range(end)]
    start = sum(counts[:begin], jnp.int32(0)) // per_chunk * per_chunk
    total = sum(counts, jnp.int32(0))
    stop = total if last else total // per_chunk * per_chunk
    before = jnp.int32(0)
    for source in range(end):

        low = jnp.clip(start - before, 0, counts[source])
        high = jnp.clip(stop - before, 0, counts[source])

        def place(step, unused, source=source, before=before, low=low, high=high):
            for extra in range(UNROLL):
                entry = jnp.minimum(low + step * UNROLL + extra, high - 1)
                code = plan_ref[source, 1 + entry]
                rows = pl.ds(pl.multiple_of((before + entry - start) * HALF, HALF), HALF)
                key_ref[rows, :] = pieces[source][code, 0]
                value_ref[rows, :HD] = pieces[source][code, 1]
                value_ref[rows, HD:] = jnp.ones((HALF, HD), jnp.bfloat16)
            return unused

        lax.fori_loop(0, (high - low + UNROLL - 1) // UNROLL, place, 0)
        before = before + counts[source]
    filled = stop - start
    chunks = (filled + per_chunk - 1) // per_chunk
    if last:

        def pad(step, unused):
            rows = pl.ds(pl.multiple_of(step * HALF, HALF), HALF)
            key_ref[rows, :] = key_ref[:HALF, :]
            value_ref[rows, :] = jnp.zeros((HALF, 2 * HD), jnp.bfloat16)
            return unused

        lax.fori_loop(filled, chunks * per_chunk, pad, 0)

    def scores_of(index, cols, step):
        rows = pl.ds(pl.multiple_of(step * CHUNK, CHUNK), CHUNK)
        return lax.dot_general(
            queries[index][:, cols], key_ref[rows, :], NT, preferred_element_type=jnp.float32
        )

    def tile_scores(tile, step):
        index, g = tiles[tile]
        return scores_of(index, slice(g * HD, (g + 1) * HD), step)

    for tile, (index, g) in enumerate(tiles):
        max_ref[tile] = state[2 * index + 1][g]
    bad_ref[0] = 1

    def attempt(number, unused):
        again = bad_ref[0] == 1

        @pl.when(again & (number == 0))
        def _():
            for index, g in tiles:
                accs[index][g] = state[2 * index][g]

        @pl.when(again & (number == 1))
        def _():
            for index in range(groups):

                def raise_max(step, unused, index=index):
                    g = step % GROUP
                    cols = pl.ds(pl.multiple_of(g * HD, HD), HD)
                    scaled = scores_of(index, cols, step // GROUP) * SCALE
                    top = jnp.max(scaled, axis=1, keepdims=True)
                    max_ref[index * GROUP + g] = jnp.maximum(max_ref[index * GROUP + g], top)
                    return unused

                def rescale(g, unused, index=index):
                    factor = jnp.exp2(state[2 * index + 1][g] - max_ref[index * GROUP + g])
                    accs[index][g] = state[2 * index][g] * jnp.concatenate([factor] * 2, axis=1)
                    return unused

                lax.fori_loop(0, chunks * GROUP, raise_max, 0)
                lax.fori_loop(0, GROUP, rescale, 0)

        @pl.when(again)
        def _():
            for tile in range(ahead):
                score_ref[tile] = tile_scores(tile, 0)

            def accumulate(step, unused):
                rows = pl.ds(pl.multiple_of(step * CHUNK, CHUNK), CHUNK)
                for tile, (index, g) in enumerate(tiles):
                    later = tile + ahead
                    coming = tile_scores(later % len(tiles), step + later // len(tiles))
                    largest = jnp.concatenate([max_ref[tile]] * (CHUNK // HD), axis=1)
                    shifted = score_ref[tile % ahead] * SCALE - largest
                    score_ref[tile % ahead] = coming
                    weights = jnp.exp2(shifted).astype(jnp.bfloat16)
                    accs[index][g] += jnp.dot(
                        weights, value_ref[rows, :], preferred_element_type=jnp.float32
                    )
                return unused

            lax.fori_loop(0, chunks, accumulate, 0)
            largest_sum = accs[0][0][:, HD:]
            for index, g in tiles[1:]:
                largest_sum = jnp.maximum(largest_sum, accs[index][g][:, HD:])
            bad_ref[0] = jnp.where(jnp.max(largest_sum) <= LIMIT, 0, 1)

        return unused

    lax.fori_loop(0, 2, attempt, 0)
    for tile, (index, g) in enumerate(tiles):
        if last:
            part = accs[0][g]
            result_ref[:, g * HD : (g + 1) * HD] = (part[:, :HD] / part[:, HD:]).astype(
                jnp.bfloat16
            )
        else:
            outs[2 * index + 1][g] = max_ref[tile]


def vertical(name, plan, parts, begin, pieces, micros, last=False):
    groups = len(parts)
    outs = STATE * groups
    scratch = []
    if last:
        outs = (jax.ShapeDtypeStruct((ROWS, COLS), jnp.bfloat16),)
        scratch = [pltpu.VMEM((GROUP, ROWS, 2 * HD), jnp.float32)]
    return pl.pallas_call(
        functools.partial(vertical_kernel, groups, begin, len(pieces), last),
        out_shape=outs,
        in_specs=[smem] + [vmem] * (3 * groups + len(pieces)),
        out_specs=(vmem,) * len(outs),
        scratch_shapes=scratch
        + [
            pltpu.VMEM((CAPACITY, HD), jnp.bfloat16),
            pltpu.VMEM((CAPACITY, 2 * HD), jnp.bfloat16),
            pltpu.VMEM((groups * GROUP, ROWS, HD), jnp.float32),
            pltpu.VMEM((2 if groups == 2 else GROUP, ROWS, CHUNK), jnp.float32),
            pltpu.SMEM((1,), jnp.int32),
        ],
        compiler_params=pltpu.CompilerParams(vmem_limit_bytes=VMEM_LIMIT),
        cost_estimate=cost(micros),
        name=name,
    )(plan, *[q for q, _ in parts], *[x for _, state in parts for x in state],
      *[piece.reshape(32, 2, HALF, HD) for piece in pieces])


def body(queries, keys, values, vert_blocks, slash_offsets):
    core = lax.axis_index("seq") & 1
    keep, send = prep(vert_blocks, keys, values)
    recv = swap(send, CORE, 1)
    keep_z = swap(keep[:, ROWS:], Z, 1)
    recv_z = cross(send[:, ROWS:])
    mine, theirs = jnp.stack([keep[:, ROWS:], keep_z]), jnp.stack([recv[:, ROWS:], recv_z])
    one = jnp.where(
        core == 0, jnp.stack([mine, theirs], axis=1), jnp.stack([theirs, mine], axis=1)
    )
    one_z = swap(one, Z, 2)
    plan = make_plan(vert_blocks, one)
    tail = jnp.where(core == 1, keep[:, :ROWS], recv[:, :ROWS])
    tail = tail + one_z[0, 0, :, :1, :1] * 0
    prev = lax.ppermute(tail, "seq", [(i, i + 2) for i in range(126)])
    own, foreign = split(queries, one)
    other = swap(foreign, CORE, 1)
    near_own = band("band_own", False, plan, slash_offsets, own, keep, recv, prev)
    near_other = band("band_other", True, plan, slash_offsets, other, keep, recv, prev)
    two = jnp.concatenate([one, one_z])
    near = []
    for part, axis in ((two[:, :, :, :HALF], Y), (two[:, :, :, HALF:], X)):
        line = jnp.stack([part, swap(part, axis, 1)])
        near.append(jnp.concatenate([line, swap(line, axis, 3)]))
    via_1 = [swap(piece, axis, 1) for piece, axis in zip(near, (X, Y))]
    via_3 = [swap(piece, axis, 3) for piece, axis in zip(near, (X, Y))]
    far = [swap(piece, axis, 1) for piece, axis in zip(via_3, (X, Y))]
    parts = ((own, near_own), (other, near_other))
    state = vertical("near", plan, parts, 0, near, 6)
    parts = ((own, state[:2]), (other, state[2:]))
    pieces = near + via_1 + via_3
    state = vertical("middle", plan, parts, 2, pieces, 12)
    pieces = pieces + far
    (foreign_result,) = vertical("far", plan, ((other, state[2:]),), 6, pieces, 4, True)
    arrived = swap(foreign_result, CORE, 1)
    (result,) = vertical("last", plan, ((own, state[:2]),), 6, pieces, 4, True)
    return jnp.where(
        core == 0,
        jnp.concatenate([result, arrived], axis=1),
        jnp.concatenate([arrived, result], axis=1),
    )


def solution(mesh):
    in_specs = (
        P("seq", "head"),
        P("seq", "head"),
        P("seq", "head"),
        P("head", None),
        P("head", None),
    )
    out_specs = P("seq", "head")
    return jax.shard_map(body, mesh=mesh, in_specs=in_specs, out_specs=out_specs, check_vma=False)
```

profile of v0, /device:TPU:31, one launch (start us, length us, event | category | flops | bytes accessed | tf_op | source)
XLA Modules:
  0.0 77.5 jit_solution(12406723123603960063)
XLA Ops:
  0.0 2.5 %prep.1 = (bf16[2,320,128]{2,1,0:T(8,128)(2,1)}, bf16[2,320,128]{2,1,0:T(8,128)(2,1)}) custom-call(s32[2,64]{1,0:T(2,128)} %vert_ref.3, bf16[256,256]{1,0:T(8,128)(2,1)} %keys_ref.1, bf16[256,256]{1,0:T(8,128)(2,1)} %values_ref.1), custom_call_target="tpu_custom_call" | custom-call | tf_op jit(solution)/shard_map/prep/pallas_call | solution.py:89
  2.5 0.7 collective-permute-start.1
  3.2 0.8 slice_bitcast_fusion.1
  3.9 1.7 %collective-permute-start = (bf16[2,64,128]{2,1,0:T(8,128)(2,1)S(1)}, bf16[2,64,128]{2,1,0:T(8,128)(2,1)S(1)}, u32[]{:S(2)}, u32[]{:S(2)}) collective-permute-start(bf16[2,64,128]{2,1,0:T(8,128)(2,1)S(1)} %get-tuple-element.40), channel_id=1, source_target_pairs={{0,4},{2,6},{4,0},{6,2},{8,12},{10,14},{12,8},{14,10},{16,20},{18,... | collective-permute-start | bytes 98312 | tf_op jit(solution)/shard_map/ppermute | solution.py:43
  5.7 0.8 slice.27
  6.4 0.0 collective-permute-start.2
  6.4 0.9 %collective-permute-done = bf16[2,64,128]{2,1,0:T(8,128)(2,1)S(1)} collective-permute-done((bf16[2,64,128]{2,1,0:T(8,128)(2,1)S(1)}, bf16[2,64,128]{2,1,0:T(8,128)(2,1)S(1)}, u32[]{:S(2)}, u32[]{:S(2)}) %collective-permute-start) | collective-permute-done | bytes 32800 | tf_op jit(solution)/shard_map/ppermute | solution.py:43
  7.3 0.0 collective-permute-done.1.recv_ref
  7.3 2.4 %collective-permute-done.2 = bf16[2,64,128]{2,1,0:T(8,128)(2,1)S(1)} collective-permute-done((bf16[2,64,128]{2,1,0:T(8,128)(2,1)S(1)}, bf16[2,64,128]{2,1,0:T(8,128)(2,1)S(1)}, u32[]{:S(2)}, u32[]{:S(2)}) %collective-permute-start.2) | collective-permute-done | bytes 32800 | tf_op jit(solution)/shard_map/ppermute | solution.py:48
  9.8 0.7 copy.16.after_ref
  10.5 3.0 %collective-permute-start.4 = (bf16[2,2,2,64,128]{4,3,2,0,1:T(8,128)(2,1)S(1)}, bf16[2,2,2,64,128]{4,3,2,0,1:T(8,128)(2,1)S(1)}, u32[]{:S(2)}, u32[]{:S(2)}) collective-permute-start(bf16[2,2,2,64,128]{4,3,2,0,1:T(8,128)(2,1)S(1)} %maximum_select_fusion.1), channel_id=1, source_target_pairs={{0,8},{2,10},{4,12},{6,14},{8,0},{10,2},{12,4},{14,6},{16,24},{18,... | collective-permute-start | bytes 393224 | tf_op jit(solution)/shard_map/ppermute | solution.py:43
  13.4 3.2 %plan.1.plan_ref.refs_0_ = s32[9,128]{1,0:T(8,128)} custom-call(s32[2,64]{1,0:T(2,128)} %vert_ref.3, bf16[2,2,2,64,128]{4,3,2,1,0:T(8,128)(2,1)} %copy.16.after_ref), custom_call_target="tpu_custom_call" | custom-call | flops 3449999872 | bytes 4194304 | tf_op jit(solution)/shard_map/plan/pallas_call | solution.py:169
  16.7 0.0 copy-start
  16.7 2.2 %split.1 = (bf16[256,896]{1,0:T(8,128)(2,1)}, bf16[256,896]{1,0:T(8,128)(2,1)}) custom-call(bf16[256,1792]{1,0:T(8,128)(2,1)} %q_ref.1, bf16[2,2,2,64,128]{4,3,2,1,0:T(8,128)(2,1)} %copy.16.after_ref), custom_call_target="tpu_custom_call" | custom-call | flops 1724999936 | bytes 4194304 | tf_op jit(solution)/shard_map/split/pallas_call | solution.py:158
  18.9 0.0 copy-start.1
  18.9 0.0 copy-start.2
  18.9 0.0 copy-start.3
  18.9 0.6 collective-permute-start.3
  19.5 0.5 collective-permute-done.4
  20.0 0.6 collective-permute-start.8
  20.7 0.5 collective-permute-start.6
  21.1 0.1 fusion.2
  21.2 0.0 copy-done
  21.2 0.1 fusion.1
  21.3 1.9 %collective-permute-start.5 = (bf16[2,256,128]{2,1,0:T(8,128)(2,1)S(1)}, bf16[2,256,128]{2,1,0:T(8,128)(2,1)S(1)}, u32[]{:S(2)}, u32[]{:S(2)}) collective-permute-start(bf16[2,256,128]{2,1,0:T(8,128)(2,1)S(1)} %fusion.1), channel_id=1, source_target_pairs={{0,4},{2,6},{4,8},{6,10},{8,12},{10,14},{12,16},{14,18},{16,20},{1... | collective-permute-start | bytes 393224 | tf_op jit(solution)/shard_map/ppermute | solution.py:421
  23.3 1.5 %collective-permute-done.8 = bf16[4,2,2,32,128]{4,3,2,0,1:T(8,128)(2,1)S(1)} collective-permute-done((bf16[4,2,2,32,128]{4,3,2,0,1:T(8,128)(2,1)S(1)}, bf16[4,2,2,32,128]{4,3,2,0,1:T(8,128)(2,1)S(1)}, u32[]{:S(2)}, u32[]{:S(2)}) %collective-permute-start.8) | collective-permute-done | bytes 131104 | tf_op jit(solution)/shard_map/ppermute | solution.py:43
  24.8 0.3 collective-permute-start.9
  25.1 0.0 collective-permute-done.6
  25.1 0.1 collective-permute-start.7
  25.2 4.5 %collective-permute-done.5.prev_ref = bf16[2,256,128]{2,1,0:T(8,128)(2,1)S(1)} collective-permute-done((bf16[2,256,128]{2,1,0:T(8,128)(2,1)S(1)}, bf16[2,256,128]{2,1,0:T(8,128)(2,1)S(1)}, u32[]{:S(2)}, u32[]{:S(2)}) %collective-permute-start.5) | collective-permute-done | bytes 131104 | tf_op jit(solution)/shard_map/ppermute | solution.py:421
  29.7 0.0 copy-done.1
  29.7 0.0 copy-done.2
  29.7 0.0 copy-done.3
  29.7 2.3 %band_own.1 = (f32[7,256,256]{2,1,0:T(8,128)S(1)}, f32[7,256,128]{2,1,0:T(8,128)S(1)}) custom-call(s32[9,128]{1,0:T(8,128)S(1)} %copy-done.3, s32[2,3]{1,0:T(2,128)S(1)} %copy-done.1, bf16[256,896]{1,0:T(8,128)(2,1)S(1)} %copy-done.2, bf16[2,320,128]{2,1,0:T(8,128)(2,1)S(1)} %copy-done, bf16[2,320,128]{2,1,0:T(8,128)(2,1)S(1)} %collective-permute-done.1.recv_ref, ...), custom_call_target="tpu_custom_call" | custom-call | flops 3449999872 | bytes 4194304 | tf_op jit(solution)/shard_map/band_own/pallas_call | solution.py:237
  32.0 0.0 collective-permute-done.3.q_ref.refs_2_.refs_1_
  32.0 2.3 %band_other.1 = (f32[7,256,256]{2,1,0:T(8,128)S(1)}, f32[7,256,128]{2,1,0:T(8,128)S(1)}) custom-call(s32[9,128]{1,0:T(8,128)S(1)} %copy-done.3, s32[2,3]{1,0:T(2,128)S(1)} %copy-done.1, bf16[256,896]{1,0:T(8,128)(2,1)S(1)} %collective-permute-done.3.q_ref.refs_2_.refs_1_, bf16[2,320,128]{2,1,0:T(8,128)(2,1)S(1)} %copy-done, ...), custom_call_target="tpu_custom_call" | custom-call | flops 3449999872 | bytes 4194304 | tf_op jit(solution)/shard_map/band_other/pallas_call | solution.py:237
  34.3 0.0 collective-permute-done.7
  34.3 0.1 pad_maximum_fusion
  34.4 1.0 %collective-permute-start.12 = (bf16[4,4,2,2,32,128]{5,4,3,1,2,0:T(8,128)(2,1)S(1)}, bf16[4,4,2,2,32,128]{5,4,3,1,2,0:T(8,128)(2,1)S(1)}, u32[]{:S(2)}, u32[]{:S(2)}) collective-permute-start(bf16[4,4,2,2,32,128]{5,4,3,1,2,0:T(8,128)(2,1)S(1)} %pad_maximum_fusion), channel_id=1, source_target_pairs={{0,192},{2,194},{4,196},{6,198},{8,200},{10,202},{12,204},{14,206}... | collective-permute-start | bytes 1572872 | tf_op jit(solution)/shard_map/ppermute | solution.py:43
  35.4 0.2 collective-permute-start.10
  35.5 0.0 collective-permute-done.9
  35.5 0.1 pad_maximum_fusion.1
  35.6 3.1 %collective-permute-start.13 = (bf16[4,4,2,2,32,128]{5,4,3,1,2,0:T(8,128)(2,1)S(1)}, bf16[4,4,2,2,32,128]{5,4,3,1,2,0:T(8,128)(2,1)S(1)}, u32[]{:S(2)}, u32[]{:S(2)}) collective-permute-start(bf16[4,4,2,2,32,128]{5,4,3,1,2,0:T(8,128)(2,1)S(1)} %pad_maximum_fusion.1), channel_id=1, source_target_pairs={{0,48},{2,50},{4,52},{6,54},{8,56},{10,58},{12,60},{14,62},{16,32}... | collective-permute-start | bytes 1572872 | tf_op jit(solution)/shard_map/ppermute | solution.py:43
  38.8 0.5 collective-permute-start.11
  39.3 5.8 %near.1 = (f32[7,256,256]{2,1,0:T(8,128)S(1)}, f32[7,256,128]{2,1,0:T(8,128)S(1)}, f32[7,256,256]{2,1,0:T(8,128)S(1)}, f32[7,256,128]{2,1,0:T(8,128)S(1)}) custom-call(s32[9,128]{1,0:T(8,128)S(1)} %copy-done.3, bf16[256,896]{1,0:T(8,128)(2,1)S(1)} %copy-done.2, bf16[256,896]{1,0:T(8,128)(2,1)S(1)} %collective-permute-done.3.q_ref.refs_2_.refs_1_, ...), custom_call_target="tpu_custom_call" | custom-call | flops 6899999744 | bytes 4194304 | tf_op jit(solution)/shard_map/near/pallas_call | solution.py:387
  45.1 1.9 %collective-permute-done.12 = bf16[4,4,2,2,32,128]{5,4,3,1,2,0:T(8,128)(2,1)S(1)} collective-permute-done((bf16[4,4,2,2,32,128]{5,4,3,1,2,0:T(8,128)(2,1)S(1)}, bf16[4,4,2,2,32,128]{5,4,3,1,2,0:T(8,128)(2,1)S(1)}, u32[]{:S(2)}, u32[]{:S(2)}) %collective-permute-start.12) | collective-permute-done | bytes 524320 | tf_op jit(solution)/shard_map/ppermute | solution.py:43
  47.0 0.1 collective-permute-start.14
  47.1 1.4 %collective-permute-done.13 = bf16[4,4,2,2,32,128]{5,4,3,1,2,0:T(8,128)(2,1)S(1)} collective-permute-done((bf16[4,4,2,2,32,128]{5,4,3,1,2,0:T(8,128)(2,1)S(1)}, bf16[4,4,2,2,32,128]{5,4,3,1,2,0:T(8,128)(2,1)S(1)}, u32[]{:S(2)}, u32[]{:S(2)}) %collective-permute-start.13) | collective-permute-done | bytes 524320 | tf_op jit(solution)/shard_map/ppermute | solution.py:43
  48.6 3.4 %collective-permute-start.15 = (bf16[4,4,2,2,32,128]{5,4,3,1,2,0:T(8,128)(2,1)S(1)}, bf16[4,4,2,2,32,128]{5,4,3,1,2,0:T(8,128)(2,1)S(1)}, u32[]{:S(2)}, u32[]{:S(2)}) collective-permute-start(bf16[4,4,2,2,32,128]{5,4,3,1,2,0:T(8,128)(2,1)S(1)} %collective-permute-done.13), channel_id=1, source_target_pairs={{0,16},{2,18},{4,20},{6,22},{8,24},{10,26},{12,28},{14,30},{16,0},... | collective-permute-start | bytes 1572872 | tf_op jit(solution)/shard_map/ppermute | solution.py:43
  52.0 0.0 collective-permute-done.10
  52.1 0.0 collective-permute-done.11
  52.1 12.1 %middle.1 = (f32[7,256,256]{2,1,0:T(8,128)S(1)}, f32[7,256,128]{2,1,0:T(8,128)S(1)}, f32[7,256,256]{2,1,0:T(8,128)S(1)}, f32[7,256,128]{2,1,0:T(8,128)S(1)}) custom-call(s32[9,128]{1,0:T(8,128)S(1)} %copy-done.3, bf16[256,896]{1,0:T(8,128)(2,1)S(1)} %copy-done.2, bf16[256,896]{1,0:T(8,128)(2,1)S(1)} %collective-permute-done.3.q_ref.refs_2_.refs_1_, ...), custom_call_target="tpu_custom_call" | custom-call | flops 13799999488 | bytes 4194304 | tf_op jit(solution)/shard_map/middle/pallas_call | solution.py:387
  64.2 0.0 collective-permute-done.14
  64.3 0.0 collective-permute-done.15
  64.3 4.0 %far.1 = bf16[256,896]{1,0:T(8,128)(2,1)S(1)} custom-call(s32[9,128]{1,0:T(8,128)S(1)} %copy-done.3, bf16[256,896]{1,0:T(8,128)(2,1)S(1)} %collective-permute-done.3.q_ref.refs_2_.refs_1_, f32[7,256,256]{2,1,0:T(8,128)S(1)} %get-tuple-element.35.refs_2_, f32[7,256,128]{2,1,0:T(8,128)S(1)} %get-tuple-element.36.refs_3_, ...), custom_call_target="tpu_custom_call" | custom-call | flops 4600000000 | bytes 4194304 | tf_op jit(solution)/shard_map/far/pallas_call | solution.py:387
  68.4 4.0 %collective-permute-start.16 = (bf16[256,896]{1,0:T(8,128)(2,1)S(1)}, bf16[256,896]{1,0:T(8,128)(2,1)S(1)}, u32[]{:S(2)}, u32[]{:S(2)}) collective-permute-start(bf16[256,896]{1,0:T(8,128)(2,1)S(1)} %far.1), channel_id=1, source_target_pairs={{0,2},{2,0},{4,6},{6,4},{8,10},{10,8},{12,14},{14,12},{16,18},{18,... | collective-permute-start | bytes 1376264 | tf_op jit(solution)/shard_map/ppermute | solution.py:43
  72.4 4.0 %last.1 = bf16[256,896]{1,0:T(8,128)(2,1)S(1)} custom-call(s32[9,128]{1,0:T(8,128)S(1)} %copy-done.3, bf16[256,896]{1,0:T(8,128)(2,1)S(1)} %copy-done.2, f32[7,256,256]{2,1,0:T(8,128)S(1)} %get-tuple-element.33.refs_2_, f32[7,256,128]{2,1,0:T(8,128)S(1)} %get-tuple-element.34.refs_3_, bf16[32,2,32,128]{3,2,1,0:T(8,128)(2,1)S(1)} %bitcast.25, ...), custom_call_target="tpu_custom_call" | custom-call | flops 4600000000 | bytes 4194304 | tf_op jit(solution)/shard_map/last/pallas_call | solution.py:387
  76.4 0.0 collective-permute-done.16
  76.4 1.1 %maximum_select_fusion = bf16[256,1792]{1,0:T(8,128)(2,1)} fusion(bf16[256,896]{1,0:T(8,128)(2,1)S(1)} %collective-permute-done.16, bf16[256,896]{1,0:T(8,128)(2,1)S(1)} %last.1, pred[]{:T(512)S(6)} %eq.7), kind=kLoop, calls=%fused_computation | loop fusion | flops 4128768 | bytes 1835009 | tf_op jit(solution)/shard_map/jit(_where)/select_n | solution.py:443
  (15 shorter events, 0.4 us)
Async XLA Ops:
  2.5 4.8 %collective-permute-start.1 = (bf16[2,320,128]{2,1,0:T(8,128)(2,1)}, bf16[2,320,128]{2,1,0:T(8,128)(2,1)S(1)}, u32[]{:S(2)}, u32[]{:S(2)}) collective-permute-start(bf16[2,320,128]{2,1,0:T(8,128)(2,1)} %get-tuple-element.22), channel_id=1, source_target_pairs={{0,2},{2,0},{4,6},{6,4},{8,10},{10,8},{12,14},{14,12},{16,18},{18,... | collective-permute-start | bytes 491528 | tf_op jit(solution)/shard_map/ppermute | solution.py:43
  3.9 3.4 %collective-permute-start = (bf16[2,64,128]{2,1,0:T(8,128)(2,1)S(1)}, bf16[2,64,128]{2,1,0:T(8,128)(2,1)S(1)}, u32[]{:S(2)}, u32[]{:S(2)}) collective-permute-start(bf16[2,64,128]{2,1,0:T(8,128)(2,1)S(1)} %get-tuple-element.40), channel_id=1, source_target_pairs={{0,4},{2,6},{4,0},{6,2},{8,12},{10,14},{12,8},{14,10},{16,20},{18,... | collective-permute-start | bytes 98312 | tf_op jit(solution)/shard_map/ppermute | solution.py:43
  6.4 3.3 %collective-permute-start.2 = (bf16[2,64,128]{2,1,0:T(8,128)(2,1)S(1)}, bf16[2,64,128]{2,1,0:T(8,128)(2,1)S(1)}, u32[]{:S(2)}, u32[]{:S(2)}) collective-permute-start(bf16[2,64,128]{2,1,0:T(8,128)(2,1)S(1)} %slice.27), channel_id=1, source_target_pairs={{0,6},{2,4},{4,2},{6,0},{8,14},{10,12},{12,10},{14,8},{16,22},{18,... | collective-permute-start | bytes 98312 | tf_op jit(solution)/shard_map/ppermute | solution.py:48
  10.5 9.6 %collective-permute-start.4 = (bf16[2,2,2,64,128]{4,3,2,0,1:T(8,128)(2,1)S(1)}, bf16[2,2,2,64,128]{4,3,2,0,1:T(8,128)(2,1)S(1)}, u32[]{:S(2)}, u32[]{:S(2)}) collective-permute-start(bf16[2,2,2,64,128]{4,3,2,0,1:T(8,128)(2,1)S(1)} %maximum_select_fusion.1), channel_id=1, source_target_pairs={{0,8},{2,10},{4,12},{6,14},{8,0},{10,2},{12,4},{14,6},{16,24},{18,... | collective-permute-start | bytes 393224 | tf_op jit(solution)/shard_map/ppermute | solution.py:43
  16.7 4.6 %copy-start = (bf16[2,320,128]{2,1,0:T(8,128)(2,1)S(1)}, bf16[2,320,128]{2,1,0:T(8,128)(2,1)}, u32[]{:S(2)}) copy-start(bf16[2,320,128]{2,1,0:T(8,128)(2,1)} %get-tuple-element.21.keep_ref) | copy-start | bytes 491524
  18.9 10.8 %copy-start.1 = (s32[2,3]{1,0:T(2,128)S(1)}, s32[2,3]{1,0:T(2,128)}, u32[]{:S(2)}) copy-start(s32[2,3]{1,0:T(2,128)} %slash_ref.3) | copy-start | bytes 76
  18.9 10.8 %copy-start.2 = (bf16[256,896]{1,0:T(8,128)(2,1)S(1)}, bf16[256,896]{1,0:T(8,128)(2,1)}, u32[]{:S(2)}) copy-start(bf16[256,896]{1,0:T(8,128)(2,1)} %get-tuple-element.23.q_ref.refs_1_) | copy-start | bytes 1376260
  18.9 10.8 %copy-start.3 = (s32[9,128]{1,0:T(8,128)S(1)}, s32[9,128]{1,0:T(8,128)}, u32[]{:S(2)}) copy-start(s32[9,128]{1,0:T(8,128)} %plan.1.plan_ref.refs_0_) | copy-start | bytes 13828
  18.9 13.1 %collective-permute-start.3 = (bf16[256,896]{1,0:T(8,128)(2,1)}, bf16[256,896]{1,0:T(8,128)(2,1)S(1)}, u32[]{:S(2)}, u32[]{:S(2)}) collective-permute-start(bf16[256,896]{1,0:T(8,128)(2,1)} %get-tuple-element.24), channel_id=1, source_target_pairs={{0,2},{2,0},{4,6},{6,4},{8,10},{10,8},{12,14},{14,12},{16,18},{18,... | collective-permute-start | bytes 1376264 | tf_op jit(solution)/shard_map/ppermute | solution.py:43
  20.0 4.7 %collective-permute-start.8 = (bf16[4,2,2,32,128]{4,3,2,0,1:T(8,128)(2,1)S(1)}, bf16[4,2,2,32,128]{4,3,2,0,1:T(8,128)(2,1)S(1)}, u32[]{:S(2)}, u32[]{:S(2)}) collective-permute-start(bf16[4,2,2,32,128]{4,3,2,0,1:T(8,128)(2,1)S(1)} %get-tuple-element.37), channel_id=1, source_target_pairs={{0,64},{2,66},{4,68},{6,70},{8,72},{10,74},{12,76},{14,78},{16,80}... | collective-permute-start | bytes 393224 | tf_op jit(solution)/shard_map/ppermute | solution.py:43
  20.7 4.4 %collective-permute-start.6 = (bf16[4,2,2,32,128]{4,3,2,0,1:T(8,128)(2,1)S(1)}, bf16[4,2,2,32,128]{4,3,2,0,1:T(8,128)(2,1)S(1)}, u32[]{:S(2)}, u32[]{:S(2)}) collective-permute-start(bf16[4,2,2,32,128]{4,3,2,0,1:T(8,128)(2,1)S(1)} %get-tuple-element.38), channel_id=1, source_target_pairs={{0,16},{2,18},{4,20},{6,22},{8,24},{10,26},{12,28},{14,30},{16,0},... | collective-permute-start | bytes 393224 | tf_op jit(solution)/shard_map/ppermute | solution.py:43
  21.3 8.4 %collective-permute-start.5 = (bf16[2,256,128]{2,1,0:T(8,128)(2,1)S(1)}, bf16[2,256,128]{2,1,0:T(8,128)(2,1)S(1)}, u32[]{:S(2)}, u32[]{:S(2)}) collective-permute-start(bf16[2,256,128]{2,1,0:T(8,128)(2,1)S(1)} %fusion.1), channel_id=1, source_target_pairs={{0,4},{2,6},{4,8},{6,10},{8,12},{10,14},{12,16},{14,18},{16,20},{1... | collective-permute-start | bytes 393224 | tf_op jit(solution)/shard_map/ppermute | solution.py:421
  24.8 10.7 %collective-permute-start.9 = (bf16[2,4,2,2,32,128]{5,4,3,1,2,0:T(8,128)(2,1)S(1)}, bf16[2,4,2,2,32,128]{5,4,3,1,2,0:T(8,128)(2,1)S(1)}, u32[]{:S(2)}, u32[]{:S(2)}) collective-permute-start(bf16[2,4,2,2,32,128]{5,4,3,1,2,0:T(8,128)(2,1)S(1)} %pad_maximum_fusion.3), channel_id=1, source_target_pairs={{0,192},{2,194},{4,196},{6,198},{8,200},{10,202},{12,204},{14,206}... | collective-permute-start | bytes 786440 | tf_op jit(solution)/shard_map/ppermute | solution.py:43
  25.1 9.2 %collective-permute-start.7 = (bf16[2,4,2,2,32,128]{5,4,3,1,2,0:T(8,128)(2,1)S(1)}, bf16[2,4,2,2,32,128]{5,4,3,1,2,0:T(8,128)(2,1)S(1)}, u32[]{:S(2)}, u32[]{:S(2)}) collective-permute-start(bf16[2,4,2,2,32,128]{5,4,3,1,2,0:T(8,128)(2,1)S(1)} %pad_maximum_fusion.2), channel_id=1, source_target_pairs={{0,48},{2,50},{4,52},{6,54},{8,56},{10,58},{12,60},{14,62},{16,32}... | collective-permute-start | bytes 786440 | tf_op jit(solution)/shard_map/ppermute | solution.py:43
  34.4 12.6 %collective-permute-start.12 = (bf16[4,4,2,2,32,128]{5,4,3,1,2,0:T(8,128)(2,1)S(1)}, bf16[4,4,2,2,32,128]{5,4,3,1,2,0:T(8,128)(2,1)S(1)}, u32[]{:S(2)}, u32[]{:S(2)}) collective-permute-start(bf16[4,4,2,2,32,128]{5,4,3,1,2,0:T(8,128)(2,1)S(1)} %pad_maximum_fusion), channel_id=1, source_target_pairs={{0,192},{2,194},{4,196},{6,198},{8,200},{10,202},{12,204},{14,206}... | collective-permute-start | bytes 1572872 | tf_op jit(solution)/shard_map/ppermute | solution.py:43
  35.4 16.6 %collective-permute-start.10 = (bf16[4,4,2,2,32,128]{5,4,3,1,2,0:T(8,128)(2,1)S(1)}, bf16[4,4,2,2,32,128]{5,4,3,1,2,0:T(8,128)(2,1)S(1)}, u32[]{:S(2)}, u32[]{:S(2)}) collective-permute-start(bf16[4,4,2,2,32,128]{5,4,3,1,2,0:T(8,128)(2,1)S(1)} %pad_maximum_fusion), channel_id=1, source_target_pairs={{0,64},{2,66},{4,68},{6,70},{8,72},{10,74},{12,76},{14,78},{16,80}... | collective-permute-start | bytes 1572872 | tf_op jit(solution)/shard_map/ppermute | solution.py:43
  35.6 12.9 %collective-permute-start.13 = (bf16[4,4,2,2,32,128]{5,4,3,1,2,0:T(8,128)(2,1)S(1)}, bf16[4,4,2,2,32,128]{5,4,3,1,2,0:T(8,128)(2,1)S(1)}, u32[]{:S(2)}, u32[]{:S(2)}) collective-permute-start(bf16[4,4,2,2,32,128]{5,4,3,1,2,0:T(8,128)(2,1)S(1)} %pad_maximum_fusion.1), channel_id=1, source_target_pairs={{0,48},{2,50},{4,52},{6,54},{8,56},{10,58},{12,60},{14,62},{16,32}... | collective-permute-start | bytes 1572872 | tf_op jit(solution)/shard_map/ppermute | solution.py:43
  38.8 13.3 %collective-permute-start.11 = (bf16[4,4,2,2,32,128]{5,4,3,1,2,0:T(8,128)(2,1)S(1)}, bf16[4,4,2,2,32,128]{5,4,3,1,2,0:T(8,128)(2,1)S(1)}, u32[]{:S(2)}, u32[]{:S(2)}) collective-permute-start(bf16[4,4,2,2,32,128]{5,4,3,1,2,0:T(8,128)(2,1)S(1)} %pad_maximum_fusion.1), channel_id=1, source_target_pairs={{0,16},{2,18},{4,20},{6,22},{8,24},{10,26},{12,28},{14,30},{16,0},... | collective-permute-start | bytes 1572872 | tf_op jit(solution)/shard_map/ppermute | solution.py:43
  47.0 17.2 %collective-permute-start.14 = (bf16[4,4,2,2,32,128]{5,4,3,1,2,0:T(8,128)(2,1)S(1)}, bf16[4,4,2,2,32,128]{5,4,3,1,2,0:T(8,128)(2,1)S(1)}, u32[]{:S(2)}, u32[]{:S(2)}) collective-permute-start(bf16[4,4,2,2,32,128]{5,4,3,1,2,0:T(8,128)(2,1)S(1)} %collective-permute-done.12), channel_id=1, source_target_pairs={{0,64},{2,66},{4,68},{6,70},{8,72},{10,74},{12,76},{14,78},{16,80}... | collective-permute-start | bytes 1572872 | tf_op jit(solution)/shard_map/ppermute | solution.py:43
  48.6 15.7 %collective-permute-start.15 = (bf16[4,4,2,2,32,128]{5,4,3,1,2,0:T(8,128)(2,1)S(1)}, bf16[4,4,2,2,32,128]{5,4,3,1,2,0:T(8,128)(2,1)S(1)}, u32[]{:S(2)}, u32[]{:S(2)}) collective-permute-start(bf16[4,4,2,2,32,128]{5,4,3,1,2,0:T(8,128)(2,1)S(1)} %collective-permute-done.13), channel_id=1, source_target_pairs={{0,16},{2,18},{4,20},{6,22},{8,24},{10,26},{12,28},{14,30},{16,0},... | collective-permute-start | bytes 1572872 | tf_op jit(solution)/shard_map/ppermute | solution.py:43
  68.4 8.0 %collective-permute-start.16 = (bf16[256,896]{1,0:T(8,128)(2,1)S(1)}, bf16[256,896]{1,0:T(8,128)(2,1)S(1)}, u32[]{:S(2)}, u32[]{:S(2)}) collective-permute-start(bf16[256,896]{1,0:T(8,128)(2,1)S(1)} %far.1), channel_id=1, source_target_pairs={{0,2},{2,0},{4,6},{6,4},{8,10},{10,8},{12,14},{14,12},{16,18},{18,... | collective-permute-start | bytes 1376264 | tf_op jit(solution)/shard_map/ppermute | solution.py:43
where the time goes:
time: 78.9 us; the launch traced here: 77.5 us
  Pallas kernels  38.3 us (49%)
  starting transfers between devices  21.7 us (28%)
  waiting for transfers between devices  13.1 us (17%)
  local copies, waits for them, and re-layouts  2.51 us (3%)
  other arithmetic  1.53 us (2%)
    pallas_call x4, Pallas kernels, vertical(): pl.pallas_call(functools.partial(vertical_kernel, groups, begin, len(piec...  25.9 us
    ppermute x15, starting transfers between devices, swap(): return lax.ppermute(block, 'seq', partner_route(axis, mask))  19.8 us
    ppermute x15, waiting for transfers between devices, swap(): return lax.ppermute(block, 'seq', partner_route(axis, mask))  6.21 us
    ppermute x1, waiting for transfers between devices, body(): prev = lax.ppermute(tail, 'seq', [(i, i + 2) for i in range(126)])  4.53 us
    pallas_call x2, Pallas kernels, band(): pl.pallas_call(functools.partial(band_kernel, foreign), out_shape=STATE,...  4.52 us
    pallas_call x1, Pallas kernels, make_plan(): pl.pallas_call(plan_kernel, out_shape=jax.ShapeDtypeStruct((9, 128), jnp....  3.23 us
    pallas_call x1, Pallas kernels, prep(): pl.pallas_call(prep_kernel, out_shape=(shape, shape), in_specs=[smem, vme...  2.48 us
    ppermute x1, waiting for transfers between devices, cross(): return lax.ppermute(block, 'seq', route)  2.41 us
  transfers between devices with their start and end apart: 17, of which 7 were waited for; matrix products, arithmetic and copies ran while one was open for 3% of the time, Pallas kernels for 41%

commit v1 on v0

--- a/solution.py
+++ b/solution.py
@@ -53,7 +53,9 @@
     return device, device >> 5, (device >> 3) & 3, (device >> 1) & 3, device & 1
 
 
-def prep_kernel(vert_ref, keys_ref, values_ref, keep_ref, send_ref):
+def prep_kernel(
+    vert_ref, keys_ref, values_ref, keep_ref, send_ref, keep_slot_ref, send_slot_ref
+):
     device, _, _, _, core = coords()
     first = device * (ROWS // BLK)
 
@@ -65,32 +67,35 @@
             out.append(jnp.where(inside, rel, found[head]))
         return tuple(out)
 
-    found = lax.fori_loop(0, NV, find, (jnp.int32(0), jnp.int32(0)))
+    found = lax.fori_loop(0, NV, find, (jnp.int32(0), jnp.int32(0)), unroll=16)
     for head in range(2):
         cols = slice(head * HD, (head + 1) * HD)
         start = pl.ds(pl.multiple_of(found[head] * BLK, BLK), BLK)
 
-        def fill(out_ref, cols=cols, start=start):
+        def fill(out_ref, slot_ref, cols=cols, start=start):
             for which, src in enumerate((keys_ref, values_ref)):
+                slot = src[start, cols]
                 out_ref[which, :ROWS] = src[:, cols]
-                out_ref[which, ROWS:] = src[start, cols]
+                out_ref[which, ROWS:] = slot
+                slot_ref[which] = slot
 
         @pl.when(core == head)
         def _(fill=fill):
-            fill(keep_ref)
+            fill(keep_ref, keep_slot_ref)
 
         @pl.when(core != head)
         def _(fill=fill):
-            fill(send_ref)
+            fill(send_ref, send_slot_ref)
 
 
 def prep(vert_blocks, keys, values):
     shape = jax.ShapeDtypeStruct((2, ROWS + BLK, HD), jnp.bfloat16)
+    slot = jax.ShapeDtypeStruct((2, BLK, HD), jnp.bfloat16)
     return pl.pallas_call(
         prep_kernel,
-        out_shape=(shape, shape),
+        out_shape=(shape, shape, slot, slot),
         in_specs=[smem, vmem, vmem],
-        out_specs=(vmem, vmem),
+        out_specs=(vmem, vmem, vmem, vmem),
         name="prep",
     )(vert_blocks, keys, values)
 
@@ -158,7 +163,7 @@
     return pl.pallas_call(
         split_kernel,
         out_shape=(shape, shape),
-        in_specs=[vmem, pl.BlockSpec(memory_space=pl.ANY)],
+        in_specs=[vmem, vmem],
         out_specs=(vmem, vmem),
         cost_estimate=cost(1.5),
         name="split",
@@ -169,7 +174,7 @@
     return pl.pallas_call(
         plan_kernel,
         out_shape=jax.ShapeDtypeStruct((9, 128), jnp.int32),
-        in_specs=[smem, pl.BlockSpec(memory_space=pl.ANY)],
+        in_specs=[smem, vmem],
         out_specs=smem,
         cost_estimate=cost(3),
         name="plan",
@@ -406,11 +411,11 @@
 
 def body(queries, keys, values, vert_blocks, slash_offsets):
     core = lax.axis_index("seq") & 1
-    keep, send = prep(vert_blocks, keys, values)
+    keep, send, keep_slot, send_slot = prep(vert_blocks, keys, values)
     recv = swap(send, CORE, 1)
-    keep_z = swap(keep[:, ROWS:], Z, 1)
-    recv_z = cross(send[:, ROWS:])
-    mine, theirs = jnp.stack([keep[:, ROWS:], keep_z]), jnp.stack([recv[:, ROWS:], recv_z])
+    keep_z = swap(keep_slot, Z, 1)
+    recv_z = cross(send_slot)
+    mine, theirs = jnp.stack([keep_slot, keep_z]), jnp.stack([recv[:, ROWS:], recv_z])
     one = jnp.where(
         core == 0, jnp.stack([mine, theirs], axis=1), jnp.stack([theirs, mine], axis=1)
     )

time: 78.9 us -> 78.7 us (level)
  Pallas kernels: 38.3 us -> 39.9 us
  local copies, waits for them, and re-layouts: 2.51 us -> 0.97 us
    ppermute x15, waiting for transfers between devices: 6.21 us -> 7.99 us  [swap(): return lax.ppermute(block, 'seq', partner_route(axis, mask))]
    ppermute x15, starting transfers between devices: 19.8 us -> 18.1 us  [swap(): return lax.ppermute(block, 'seq', partner_route(axis, mask))]
    pallas_call x4, Pallas kernels: 25.9 us -> 27.6 us  [vertical(): pl.pallas_call(functools.partial(vertical_kernel, groups, begin, len(piec...]
    ppermute x1, waiting for transfers between devices: 2.41 us -> 1.28 us  [cross(): return lax.ppermute(block, 'seq', route)]
    ppermute x1, starting transfers between devices: 1.92 us -> 3 us  [body(): prev = lax.ppermute(tail, 'seq', [(i, i + 2) for i in range(126)])]
    ppermute x1, waiting for transfers between devices: 4.53 us -> 3.51 us  [body(): prev = lax.ppermute(tail, 'seq', [(i, i + 2) for i in range(126)])]
  transfers between devices with their start and end apart: 17 -> 17, of which waited for: 7 -> 8; matrix products, arithmetic and copies ran while one was open for 3% -> 2% of each run, Pallas kernels for 41% -> 42%
where the time goes in v1:
time: 78.7 us; the launch traced here: 77.3 us
  Pallas kernels  39.9 us (51%)
  starting transfers between devices  21.1 us (27%)
  waiting for transfers between devices  12.8 us (16%)
  other arithmetic  2.29 us (3%)
  local copies, waits for them, and re-layouts  0.97 us (1%)
    pallas_call x4, Pallas kernels, vertical(): pl.pallas_call(functools.partial(vertical_kernel, groups, begin, len(piec...  27.6 us
    ppermute x15, starting transfers between devices, swap(): return lax.ppermute(block, 'seq', partner_route(axis, mask))  18.1 us
    ppermute x15, waiting for transfers between devices, swap(): return lax.ppermute(block, 'seq', partner_route(axis, mask))  7.99 us
    pallas_call x2, Pallas kernels, band(): pl.pallas_call(functools.partial(band_kernel, foreign), out_shape=STATE,...  4.53 us
    ppermute x1, waiting for transfers between devices, body(): prev = lax.ppermute(tail, 'seq', [(i, i + 2) for i in range(126)])  3.51 us
    pallas_call x1, Pallas kernels, make_plan(): pl.pallas_call(plan_kernel, out_shape=jax.ShapeDtypeStruct((9, 128), jnp....  3.45 us
    ppermute x1, starting transfers between devices, body(): prev = lax.ppermute(tail, 'seq', [(i, i + 2) for i in range(126)])  3 us
    pallas_call x1, Pallas kernels, split(): pl.pallas_call(split_kernel, out_shape=(shape, shape), in_specs=[vmem, vm...  2.21 us
  transfers between devices with their start and end apart: 17, of which 8 were waited for; matrix products, arithmetic and copies ran while one was open for 2% of the time, Pallas kernels for 42%

profile of v1, /device:TPU:31, one launch (start us, length us, event | category | flops | bytes accessed | tf_op | source)
XLA Modules:
  0.0 77.3 jit_solution(3723986829798833039)
XLA Ops:
  0.0 2.1 %prep.1 = (bf16[2,320,128]{2,1,0:T(8,128)(2,1)}, bf16[2,320,128]{2,1,0:T(8,128)(2,1)}, bf16[2,64,128]{2,1,0:T(8,128)(2,1)}, bf16[2,64,128]{2,1,0:T(8,128)(2,1)}) custom-call(s32[2,64]{1,0:T(2,128)} %vert_ref.3, bf16[256,256]{1,0:T(8,128)(2,1)} %keys_ref.1, bf16[256,256]{1,0:T(8,128)(2,1)} %values_ref.1), custom_call_target="tpu_custom_call" | custom-call | tf_op jit(solution)/shard_map/prep/pallas_call | solution.py:94
  2.1 0.7 collective-permute-start.1
  2.8 1.7 %collective-permute-start = (bf16[2,64,128]{2,1,0:T(8,128)(2,1)}, bf16[2,64,128]{2,1,0:T(8,128)(2,1)S(1)}, u32[]{:S(2)}, u32[]{:S(2)}) collective-permute-start(bf16[2,64,128]{2,1,0:T(8,128)(2,1)} %get-tuple-element.23), channel_id=1, source_target_pairs={{0,4},{2,6},{4,0},{6,2},{8,12},{10,14},{12,8},{14,10},{16,20},{18,... | collective-permute-start | bytes 98312 | tf_op jit(solution)/shard_map/ppermute | solution.py:43
  4.4 0.1 collective-permute-start.2
  4.5 1.4 %collective-permute-done = bf16[2,64,128]{2,1,0:T(8,128)(2,1)S(1)} collective-permute-done((bf16[2,64,128]{2,1,0:T(8,128)(2,1)}, bf16[2,64,128]{2,1,0:T(8,128)(2,1)S(1)}, u32[]{:S(2)}, u32[]{:S(2)}) %collective-permute-start) | collective-permute-done | bytes 32800 | tf_op jit(solution)/shard_map/ppermute | solution.py:43
  5.9 0.8 maximum_bitcast_fusion
  6.7 0.0 collective-permute-done.1.recv_ref
  6.7 1.3 %collective-permute-done.2 = bf16[2,64,128]{2,1,0:T(8,128)(2,1)S(1)} collective-permute-done((bf16[2,64,128]{2,1,0:T(8,128)(2,1)}, bf16[2,64,128]{2,1,0:T(8,128)(2,1)S(1)}, u32[]{:S(2)}, u32[]{:S(2)}) %collective-permute-start.2) | collective-permute-done | bytes 32800 | tf_op jit(solution)/shard_map/ppermute | solution.py:48
  8.0 0.7 copy.16.after_ref
  8.7 3.0 %collective-permute-start.4 = (bf16[2,2,2,64,128]{4,3,2,0,1:T(8,128)(2,1)S(1)}, bf16[2,2,2,64,128]{4,3,2,0,1:T(8,128)(2,1)S(1)}, u32[]{:S(2)}, u32[]{:S(2)}) collective-permute-start(bf16[2,2,2,64,128]{4,3,2,0,1:T(8,128)(2,1)S(1)} %maximum_select_fusion.1), channel_id=1, source_target_pairs={{0,8},{2,10},{4,12},{6,14},{8,0},{10,2},{12,4},{14,6},{16,24},{18,... | collective-permute-start | bytes 393224 | tf_op jit(solution)/shard_map/ppermute | solution.py:43
  11.7 3.5 %plan.1.plan_ref.refs_0_ = s32[9,128]{1,0:T(8,128)} custom-call(s32[2,64]{1,0:T(2,128)} %vert_ref.3, bf16[2,2,2,64,128]{4,3,2,1,0:T(8,128)(2,1)} %copy.16.after_ref), custom_call_target="tpu_custom_call" | custom-call | flops 3449999872 | bytes 4194304 | tf_op jit(solution)/shard_map/plan/pallas_call | solution.py:174
  15.1 0.0 copy-start
  15.2 2.2 %split.1 = (bf16[256,896]{1,0:T(8,128)(2,1)}, bf16[256,896]{1,0:T(8,128)(2,1)}) custom-call(bf16[256,1792]{1,0:T(8,128)(2,1)} %q_ref.1, bf16[2,2,2,64,128]{4,3,2,1,0:T(8,128)(2,1)} %copy.16.after_ref), custom_call_target="tpu_custom_call" | custom-call | flops 1724999936 | bytes 4194304 | tf_op jit(solution)/shard_map/split/pallas_call | solution.py:163
  17.4 0.0 copy-start.1
  17.4 0.0 copy-start.2
  17.4 0.0 copy-start.3
  17.4 0.7 collective-permute-start.3
  18.1 0.2 collective-permute-done.4
  18.3 0.6 collective-permute-start.8
  18.9 0.5 collective-permute-start.6
  19.4 0.1 fusion.2
  19.5 0.0 copy-done
  19.5 0.1 fusion.1
  19.6 3.0 %collective-permute-start.5 = (bf16[2,256,128]{2,1,0:T(8,128)(2,1)S(1)}, bf16[2,256,128]{2,1,0:T(8,128)(2,1)S(1)}, u32[]{:S(2)}, u32[]{:S(2)}) collective-permute-start(bf16[2,256,128]{2,1,0:T(8,128)(2,1)S(1)} %fusion.1), channel_id=1, source_target_pairs={{0,4},{2,6},{4,8},{6,10},{8,12},{10,14},{12,16},{14,18},{16,20},{1... | collective-permute-start | bytes 393224 | tf_op jit(solution)/shard_map/ppermute | solution.py:426
  22.6 0.2 collective-permute-done.8
  22.8 0.8 %collective-permute-start.9 = (bf16[2,4,2,2,32,128]{5,4,3,1,2,0:T(8,128)(2,1)S(1)}, bf16[2,4,2,2,32,128]{5,4,3,1,2,0:T(8,128)(2,1)S(1)}, u32[]{:S(2)}, u32[]{:S(2)}) collective-permute-start(bf16[2,4,2,2,32,128]{5,4,3,1,2,0:T(8,128)(2,1)S(1)} %pad_maximum_fusion.3), channel_id=1, source_target_pairs={{0,192},{2,194},{4,196},{6,198},{8,200},{10,202},{12,204},{14,206}... | collective-permute-start | bytes 786440 | tf_op jit(solution)/shard_map/ppermute | solution.py:43
  23.6 0.0 collective-permute-done.6
  23.6 0.9 %collective-permute-start.7 = (bf16[2,4,2,2,32,128]{5,4,3,1,2,0:T(8,128)(2,1)S(1)}, bf16[2,4,2,2,32,128]{5,4,3,1,2,0:T(8,128)(2,1)S(1)}, u32[]{:S(2)}, u32[]{:S(2)}) collective-permute-start(bf16[2,4,2,2,32,128]{5,4,3,1,2,0:T(8,128)(2,1)S(1)} %pad_maximum_fusion.2), channel_id=1, source_target_pairs={{0,48},{2,50},{4,52},{6,54},{8,56},{10,58},{12,60},{14,62},{16,32}... | collective-permute-start | bytes 786440 | tf_op jit(solution)/shard_map/ppermute | solution.py:43
  24.5 3.5 %collective-permute-done.5.prev_ref = bf16[2,256,128]{2,1,0:T(8,128)(2,1)S(1)} collective-permute-done((bf16[2,256,128]{2,1,0:T(8,128)(2,1)S(1)}, bf16[2,256,128]{2,1,0:T(8,128)(2,1)S(1)}, u32[]{:S(2)}, u32[]{:S(2)}) %collective-permute-start.5) | collective-permute-done | bytes 131104 | tf_op jit(solution)/shard_map/ppermute | solution.py:426
  28.0 0.0 copy-done.1
  28.0 0.0 copy-done.2
  28.0 0.0 copy-done.3
  28.0 2.3 %band_own.1 = (f32[7,256,256]{2,1,0:T(8,128)S(1)}, f32[7,256,128]{2,1,0:T(8,128)S(1)}) custom-call(s32[9,128]{1,0:T(8,128)S(1)} %copy-done.3, s32[2,3]{1,0:T(2,128)S(1)} %copy-done.1, bf16[256,896]{1,0:T(8,128)(2,1)S(1)} %copy-done.2, bf16[2,320,128]{2,1,0:T(8,128)(2,1)S(1)} %copy-done, bf16[2,320,128]{2,1,0:T(8,128)(2,1)S(1)} %collective-permute-done.1.recv_ref, ...), custom_call_target="tpu_custom_call" | custom-call | flops 3449999872 | bytes 4194304 | tf_op jit(solution)/shard_map/band_own/pallas_call | solution.py:242
  30.3 0.0 collective-permute-done.3.q_ref.refs_2_.refs_1_
  30.3 2.3 %band_other.1 = (f32[7,256,256]{2,1,0:T(8,128)S(1)}, f32[7,256,128]{2,1,0:T(8,128)S(1)}) custom-call(s32[9,128]{1,0:T(8,128)S(1)} %copy-done.3, s32[2,3]{1,0:T(2,128)S(1)} %copy-done.1, bf16[256,896]{1,0:T(8,128)(2,1)S(1)} %collective-permute-done.3.q_ref.refs_2_.refs_1_, bf16[2,320,128]{2,1,0:T(8,128)(2,1)S(1)} %copy-done, ...), custom_call_target="tpu_custom_call" | custom-call | flops 3449999872 | bytes 4194304 | tf_op jit(solution)/shard_map/band_other/pallas_call | solution.py:242
  32.6 0.0 collective-permute-done.7
  32.6 0.1 pad_maximum_fusion
  32.7 0.9 %collective-permute-start.12 = (bf16[4,4,2,2,32,128]{5,4,3,1,2,0:T(8,128)(2,1)S(1)}, bf16[4,4,2,2,32,128]{5,4,3,1,2,0:T(8,128)(2,1)S(1)}, u32[]{:S(2)}, u32[]{:S(2)}) collective-permute-start(bf16[4,4,2,2,32,128]{5,4,3,1,2,0:T(8,128)(2,1)S(1)} %pad_maximum_fusion), channel_id=1, source_target_pairs={{0,192},{2,194},{4,196},{6,198},{8,200},{10,202},{12,204},{14,206}... | collective-permute-start | bytes 1572872 | tf_op jit(solution)/shard_map/ppermute | solution.py:43
  33.6 1.0 %collective-permute-start.10 = (bf16[4,4,2,2,32,128]{5,4,3,1,2,0:T(8,128)(2,1)S(1)}, bf16[4,4,2,2,32,128]{5,4,3,1,2,0:T(8,128)(2,1)S(1)}, u32[]{:S(2)}, u32[]{:S(2)}) collective-permute-start(bf16[4,4,2,2,32,128]{5,4,3,1,2,0:T(8,128)(2,1)S(1)} %pad_maximum_fusion), channel_id=1, source_target_pairs={{0,64},{2,66},{4,68},{6,70},{8,72},{10,74},{12,76},{14,78},{16,80}... | collective-permute-start | bytes 1572872 | tf_op jit(solution)/shard_map/ppermute | solution.py:43
  34.6 0.0 collective-permute-done.9
  34.6 0.1 pad_maximum_fusion.1
  34.7 3.5 %collective-permute-start.13 = (bf16[4,4,2,2,32,128]{5,4,3,1,2,0:T(8,128)(2,1)S(1)}, bf16[4,4,2,2,32,128]{5,4,3,1,2,0:T(8,128)(2,1)S(1)}, u32[]{:S(2)}, u32[]{:S(2)}) collective-permute-start(bf16[4,4,2,2,32,128]{5,4,3,1,2,0:T(8,128)(2,1)S(1)} %pad_maximum_fusion.1), channel_id=1, source_target_pairs={{0,48},{2,50},{4,52},{6,54},{8,56},{10,58},{12,60},{14,62},{16,32}... | collective-permute-start | bytes 1572872 | tf_op jit(solution)/shard_map/ppermute | solution.py:43
  38.2 0.0 collective-permute-start.11
  38.2 4.5 %near.1 = (f32[7,256,256]{2,1,0:T(8,128)S(1)}, f32[7,256,128]{2,1,0:T(8,128)S(1)}, f32[7,256,256]{2,1,0:T(8,128)S(1)}, f32[7,256,128]{2,1,0:T(8,128)S(1)}) custom-call(s32[9,128]{1,0:T(8,128)S(1)} %copy-done.3, bf16[256,896]{1,0:T(8,128)(2,1)S(1)} %copy-done.2, bf16[256,896]{1,0:T(8,128)(2,1)S(1)} %collective-permute-done.3.q_ref.refs_2_.refs_1_, ...), custom_call_target="tpu_custom_call" | custom-call | flops 6899999744 | bytes 4194304 | tf_op jit(solution)/shard_map/near/pallas_call | solution.py:392
  42.7 2.3 %collective-permute-done.12 = bf16[4,4,2,2,32,128]{5,4,3,1,2,0:T(8,128)(2,1)S(1)} collective-permute-done((bf16[4,4,2,2,32,128]{5,4,3,1,2,0:T(8,128)(2,1)S(1)}, bf16[4,4,2,2,32,128]{5,4,3,1,2,0:T(8,128)(2,1)S(1)}, u32[]{:S(2)}, u32[]{:S(2)}) %collective-permute-start.12) | collective-permute-done | bytes 524320 | tf_op jit(solution)/shard_map/ppermute | solution.py:43
  45.0 0.1 collective-permute-start.14
  45.1 3.8 %collective-permute-done.13 = bf16[4,4,2,2,32,128]{5,4,3,1,2,0:T(8,128)(2,1)S(1)} collective-permute-done((bf16[4,4,2,2,32,128]{5,4,3,1,2,0:T(8,128)(2,1)S(1)}, bf16[4,4,2,2,32,128]{5,4,3,1,2,0:T(8,128)(2,1)S(1)}, u32[]{:S(2)}, u32[]{:S(2)}) %collective-permute-start.13) | collective-permute-done | bytes 524320 | tf_op jit(solution)/shard_map/ppermute | solution.py:43
  49.0 0.7 collective-permute-start.15
  49.7 0.0 collective-permute-done.10
  49.8 0.1 collective-permute-done.11
  49.9 12.1 %middle.1 = (f32[7,256,256]{2,1,0:T(8,128)S(1)}, f32[7,256,128]{2,1,0:T(8,128)S(1)}, f32[7,256,256]{2,1,0:T(8,128)S(1)}, f32[7,256,128]{2,1,0:T(8,128)S(1)}) custom-call(s32[9,128]{1,0:T(8,128)S(1)} %copy-done.3, bf16[256,896]{1,0:T(8,128)(2,1)S(1)} %copy-done.2, bf16[256,896]{1,0:T(8,128)(2,1)S(1)} %collective-permute-done.3.q_ref.refs_2_.refs_1_, ...), custom_call_target="tpu_custom_call" | custom-call | flops 13799999488 | bytes 4194304 | tf_op jit(solution)/shard_map/middle/pallas_call | solution.py:392
  62.0 0.0 collective-permute-done.14
  62.1 0.0 collective-permute-done.15
  62.2 5.5 %far.1 = bf16[256,896]{1,0:T(8,128)(2,1)S(1)} custom-call(s32[9,128]{1,0:T(8,128)S(1)} %copy-done.3, bf16[256,896]{1,0:T(8,128)(2,1)S(1)} %collective-permute-done.3.q_ref.refs_2_.refs_1_, f32[7,256,256]{2,1,0:T(8,128)S(1)} %get-tuple-element.39.refs_2_, f32[7,256,128]{2,1,0:T(8,128)S(1)} %get-tuple-element.40.refs_3_, ...), custom_call_target="tpu_custom_call" | custom-call | flops 4600000000 | bytes 4194304 | tf_op jit(solution)/shard_map/far/pallas_call | solution.py:392
  67.6 3.0 %collective-permute-start.16 = (bf16[256,896]{1,0:T(8,128)(2,1)S(1)}, bf16[256,896]{1,0:T(8,128)(2,1)S(1)}, u32[]{:S(2)}, u32[]{:S(2)}) collective-permute-start(bf16[256,896]{1,0:T(8,128)(2,1)S(1)} %far.1), channel_id=1, source_target_pairs={{0,2},{2,0},{4,6},{6,4},{8,10},{10,8},{12,14},{14,12},{16,18},{18,... | collective-permute-start | bytes 1376264 | tf_op jit(solution)/shard_map/ppermute | solution.py:43
  70.7 5.5 %last.1 = bf16[256,896]{1,0:T(8,128)(2,1)S(1)} custom-call(s32[9,128]{1,0:T(8,128)S(1)} %copy-done.3, bf16[256,896]{1,0:T(8,128)(2,1)S(1)} %copy-done.2, f32[7,256,256]{2,1,0:T(8,128)S(1)} %get-tuple-element.37.refs_2_, f32[7,256,128]{2,1,0:T(8,128)S(1)} %get-tuple-element.38.refs_3_, bf16[32,2,32,128]{3,2,1,0:T(8,128)(2,1)S(1)} %bitcast.24, ...), custom_call_target="tpu_custom_call" | custom-call | flops 4600000000 | bytes 4194304 | tf_op jit(solution)/shard_map/last/pallas_call | solution.py:392
  76.1 0.0 collective-permute-done.16
  76.2 1.1 %maximum_select_fusion = bf16[256,1792]{1,0:T(8,128)(2,1)} fusion(bf16[256,896]{1,0:T(8,128)(2,1)S(1)} %collective-permute-done.16, bf16[256,896]{1,0:T(8,128)(2,1)S(1)} %last.1, pred[]{:T(512)S(6)} %eq.7), kind=kLoop, calls=%fused_computation | loop fusion | flops 4128768 | bytes 1835009 | tf_op jit(solution)/shard_map/jit(_where)/select_n | solution.py:448
  (14 shorter events, 0.4 us)
Async XLA Ops:
  2.1 4.6 %collective-permute-start.1 = (bf16[2,320,128]{2,1,0:T(8,128)(2,1)}, bf16[2,320,128]{2,1,0:T(8,128)(2,1)S(1)}, u32[]{:S(2)}, u32[]{:S(2)}) collective-permute-start(bf16[2,320,128]{2,1,0:T(8,128)(2,1)} %get-tuple-element.24), channel_id=1, source_target_pairs={{0,2},{2,0},{4,6},{6,4},{8,10},{10,8},{12,14},{14,12},{16,18},{18,... | collective-permute-start | bytes 491528 | tf_op jit(solution)/shard_map/ppermute | solution.py:43
  2.8 3.1 %collective-permute-start = (bf16[2,64,128]{2,1,0:T(8,128)(2,1)}, bf16[2,64,128]{2,1,0:T(8,128)(2,1)S(1)}, u32[]{:S(2)}, u32[]{:S(2)}) collective-permute-start(bf16[2,64,128]{2,1,0:T(8,128)(2,1)} %get-tuple-element.23), channel_id=1, source_target_pairs={{0,4},{2,6},{4,0},{6,2},{8,12},{10,14},{12,8},{14,10},{16,20},{18,... | collective-permute-start | bytes 98312 | tf_op jit(solution)/shard_map/ppermute | solution.py:43
  4.4 3.6 %collective-permute-start.2 = (bf16[2,64,128]{2,1,0:T(8,128)(2,1)}, bf16[2,64,128]{2,1,0:T(8,128)(2,1)S(1)}, u32[]{:S(2)}, u32[]{:S(2)}) collective-permute-start(bf16[2,64,128]{2,1,0:T(8,128)(2,1)} %get-tuple-element.25), channel_id=1, source_target_pairs={{0,6},{2,4},{4,2},{6,0},{8,14},{10,12},{12,10},{14,8},{16,22},{18,... | collective-permute-start | bytes 98312 | tf_op jit(solution)/shard_map/ppermute | solution.py:48
  8.7 9.6 %collective-permute-start.4 = (bf16[2,2,2,64,128]{4,3,2,0,1:T(8,128)(2,1)S(1)}, bf16[2,2,2,64,128]{4,3,2,0,1:T(8,128)(2,1)S(1)}, u32[]{:S(2)}, u32[]{:S(2)}) collective-permute-start(bf16[2,2,2,64,128]{4,3,2,0,1:T(8,128)(2,1)S(1)} %maximum_select_fusion.1), channel_id=1, source_target_pairs={{0,8},{2,10},{4,12},{6,14},{8,0},{10,2},{12,4},{14,6},{16,24},{18,... | collective-permute-start | bytes 393224 | tf_op jit(solution)/shard_map/ppermute | solution.py:43
  15.1 4.3 %copy-start = (bf16[2,320,128]{2,1,0:T(8,128)(2,1)S(1)}, bf16[2,320,128]{2,1,0:T(8,128)(2,1)}, u32[]{:S(2)}) copy-start(bf16[2,320,128]{2,1,0:T(8,128)(2,1)} %get-tuple-element.28.keep_ref) | copy-start | bytes 491524
  17.4 10.6 %copy-start.1 = (s32[2,3]{1,0:T(2,128)S(1)}, s32[2,3]{1,0:T(2,128)}, u32[]{:S(2)}) copy-start(s32[2,3]{1,0:T(2,128)} %slash_ref.3) | copy-start | bytes 76
  17.4 10.6 %copy-start.2 = (bf16[256,896]{1,0:T(8,128)(2,1)S(1)}, bf16[256,896]{1,0:T(8,128)(2,1)}, u32[]{:S(2)}) copy-start(bf16[256,896]{1,0:T(8,128)(2,1)} %get-tuple-element.26.q_ref.refs_1_) | copy-start | bytes 1376260
  17.4 10.6 %copy-start.3 = (s32[9,128]{1,0:T(8,128)S(1)}, s32[9,128]{1,0:T(8,128)}, u32[]{:S(2)}) copy-start(s32[9,128]{1,0:T(8,128)} %plan.1.plan_ref.refs_0_) | copy-start | bytes 13828
  17.4 12.9 %collective-permute-start.3 = (bf16[256,896]{1,0:T(8,128)(2,1)}, bf16[256,896]{1,0:T(8,128)(2,1)S(1)}, u32[]{:S(2)}, u32[]{:S(2)}) collective-permute-start(bf16[256,896]{1,0:T(8,128)(2,1)} %get-tuple-element.27), channel_id=1, source_target_pairs={{0,2},{2,0},{4,6},{6,4},{8,10},{10,8},{12,14},{14,12},{16,18},{18,... | collective-permute-start | bytes 1376264 | tf_op jit(solution)/shard_map/ppermute | solution.py:43
  18.3 4.4 %collective-permute-start.8 = (bf16[4,2,2,32,128]{4,3,2,0,1:T(8,128)(2,1)S(1)}, bf16[4,2,2,32,128]{4,3,2,0,1:T(8,128)(2,1)S(1)}, u32[]{:S(2)}, u32[]{:S(2)}) collective-permute-start(bf16[4,2,2,32,128]{4,3,2,0,1:T(8,128)(2,1)S(1)} %get-tuple-element.41), channel_id=1, source_target_pairs={{0,64},{2,66},{4,68},{6,70},{8,72},{10,74},{12,76},{14,78},{16,80}... | collective-permute-start | bytes 393224 | tf_op jit(solution)/shard_map/ppermute | solution.py:43
  18.9 4.7 %collective-permute-start.6 = (bf16[4,2,2,32,128]{4,3,2,0,1:T(8,128)(2,1)S(1)}, bf16[4,2,2,32,128]{4,3,2,0,1:T(8,128)(2,1)S(1)}, u32[]{:S(2)}, u32[]{:S(2)}) collective-permute-start(bf16[4,2,2,32,128]{4,3,2,0,1:T(8,128)(2,1)S(1)} %get-tuple-element.42), channel_id=1, source_target_pairs={{0,16},{2,18},{4,20},{6,22},{8,24},{10,26},{12,28},{14,30},{16,0},... | collective-permute-start | bytes 393224 | tf_op jit(solution)/shard_map/ppermute | solution.py:43
  19.6 8.4 %collective-permute-start.5 = (bf16[2,256,128]{2,1,0:T(8,128)(2,1)S(1)}, bf16[2,256,128]{2,1,0:T(8,128)(2,1)S(1)}, u32[]{:S(2)}, u32[]{:S(2)}) collective-permute-start(bf16[2,256,128]{2,1,0:T(8,128)(2,1)S(1)} %fusion.1), channel_id=1, source_target_pairs={{0,4},{2,6},{4,8},{6,10},{8,12},{10,14},{12,16},{14,18},{16,20},{1... | collective-permute-start | bytes 393224 | tf_op jit(solution)/shard_map/ppermute | solution.py:426
  22.8 11.8 %collective-permute-start.9 = (bf16[2,4,2,2,32,128]{5,4,3,1,2,0:T(8,128)(2,1)S(1)}, bf16[2,4,2,2,32,128]{5,4,3,1,2,0:T(8,128)(2,1)S(1)}, u32[]{:S(2)}, u32[]{:S(2)}) collective-permute-start(bf16[2,4,2,2,32,128]{5,4,3,1,2,0:T(8,128)(2,1)S(1)} %pad_maximum_fusion.3), channel_id=1, source_target_pairs={{0,192},{2,194},{4,196},{6,198},{8,200},{10,202},{12,204},{14,206}... | collective-permute-start | bytes 786440 | tf_op jit(solution)/shard_map/ppermute | solution.py:43
  23.6 8.9 %collective-permute-start.7 = (bf16[2,4,2,2,32,128]{5,4,3,1,2,0:T(8,128)(2,1)S(1)}, bf16[2,4,2,2,32,128]{5,4,3,1,2,0:T(8,128)(2,1)S(1)}, u32[]{:S(2)}, u32[]{:S(2)}) collective-permute-start(bf16[2,4,2,2,32,128]{5,4,3,1,2,0:T(8,128)(2,1)S(1)} %pad_maximum_fusion.2), channel_id=1, source_target_pairs={{0,48},{2,50},{4,52},{6,54},{8,56},{10,58},{12,60},{14,62},{16,32}... | collective-permute-start | bytes 786440 | tf_op jit(solution)/shard_map/ppermute | solution.py:43
  32.7 12.3 %collective-permute-start.12 = (bf16[4,4,2,2,32,128]{5,4,3,1,2,0:T(8,128)(2,1)S(1)}, bf16[4,4,2,2,32,128]{5,4,3,1,2,0:T(8,128)(2,1)S(1)}, u32[]{:S(2)}, u32[]{:S(2)}) collective-permute-start(bf16[4,4,2,2,32,128]{5,4,3,1,2,0:T(8,128)(2,1)S(1)} %pad_maximum_fusion), channel_id=1, source_target_pairs={{0,192},{2,194},{4,196},{6,198},{8,200},{10,202},{12,204},{14,206}... | collective-permute-start | bytes 1572872 | tf_op jit(solution)/shard_map/ppermute | solution.py:43
  33.6 16.1 %collective-permute-start.10 = (bf16[4,4,2,2,32,128]{5,4,3,1,2,0:T(8,128)(2,1)S(1)}, bf16[4,4,2,2,32,128]{5,4,3,1,2,0:T(8,128)(2,1)S(1)}, u32[]{:S(2)}, u32[]{:S(2)}) collective-permute-start(bf16[4,4,2,2,32,128]{5,4,3,1,2,0:T(8,128)(2,1)S(1)} %pad_maximum_fusion), channel_id=1, source_target_pairs={{0,64},{2,66},{4,68},{6,70},{8,72},{10,74},{12,76},{14,78},{16,80}... | collective-permute-start | bytes 1572872 | tf_op jit(solution)/shard_map/ppermute | solution.py:43
  34.7 14.3 %collective-permute-start.13 = (bf16[4,4,2,2,32,128]{5,4,3,1,2,0:T(8,128)(2,1)S(1)}, bf16[4,4,2,2,32,128]{5,4,3,1,2,0:T(8,128)(2,1)S(1)}, u32[]{:S(2)}, u32[]{:S(2)}) collective-permute-start(bf16[4,4,2,2,32,128]{5,4,3,1,2,0:T(8,128)(2,1)S(1)} %pad_maximum_fusion.1), channel_id=1, source_target_pairs={{0,48},{2,50},{4,52},{6,54},{8,56},{10,58},{12,60},{14,62},{16,32}... | collective-permute-start | bytes 1572872 | tf_op jit(solution)/shard_map/ppermute | solution.py:43
  38.2 11.7 %collective-permute-start.11 = (bf16[4,4,2,2,32,128]{5,4,3,1,2,0:T(8,128)(2,1)S(1)}, bf16[4,4,2,2,32,128]{5,4,3,1,2,0:T(8,128)(2,1)S(1)}, u32[]{:S(2)}, u32[]{:S(2)}) collective-permute-start(bf16[4,4,2,2,32,128]{5,4,3,1,2,0:T(8,128)(2,1)S(1)} %pad_maximum_fusion.1), channel_id=1, source_target_pairs={{0,16},{2,18},{4,20},{6,22},{8,24},{10,26},{12,28},{14,30},{16,0},... | collective-permute-start | bytes 1572872 | tf_op jit(solution)/shard_map/ppermute | solution.py:43
  45.0 17.0 %collective-permute-start.14 = (bf16[4,4,2,2,32,128]{5,4,3,1,2,0:T(8,128)(2,1)S(1)}, bf16[4,4,2,2,32,128]{5,4,3,1,2,0:T(8,128)(2,1)S(1)}, u32[]{:S(2)}, u32[]{:S(2)}) collective-permute-start(bf16[4,4,2,2,32,128]{5,4,3,1,2,0:T(8,128)(2,1)S(1)} %collective-permute-done.12), channel_id=1, source_target_pairs={{0,64},{2,66},{4,68},{6,70},{8,72},{10,74},{12,76},{14,78},{16,80}... | collective-permute-start | bytes 1572872 | tf_op jit(solution)/shard_map/ppermute | solution.py:43
  49.0 13.1 %collective-permute-start.15 = (bf16[4,4,2,2,32,128]{5,4,3,1,2,0:T(8,128)(2,1)S(1)}, bf16[4,4,2,2,32,128]{5,4,3,1,2,0:T(8,128)(2,1)S(1)}, u32[]{:S(2)}, u32[]{:S(2)}) collective-permute-start(bf16[4,4,2,2,32,128]{5,4,3,1,2,0:T(8,128)(2,1)S(1)} %collective-permute-done.13), channel_id=1, source_target_pairs={{0,16},{2,18},{4,20},{6,22},{8,24},{10,26},{12,28},{14,30},{16,0},... | collective-permute-start | bytes 1572872 | tf_op jit(solution)/shard_map/ppermute | solution.py:43
  67.6 8.5 %collective-permute-start.16 = (bf16[256,896]{1,0:T(8,128)(2,1)S(1)}, bf16[256,896]{1,0:T(8,128)(2,1)S(1)}, u32[]{:S(2)}, u32[]{:S(2)}) collective-permute-start(bf16[256,896]{1,0:T(8,128)(2,1)S(1)} %far.1), channel_id=1, source_target_pairs={{0,2},{2,0},{4,6},{6,4},{8,10},{10,8},{12,14},{14,12},{16,18},{18,... | collective-permute-start | bytes 1376264 | tf_op jit(solution)/shard_map/ppermute | solution.py:43

commit v2 on v1

--- a/solution.py
+++ b/solution.py
@@ -420,11 +420,12 @@
         core == 0, jnp.stack([mine, theirs], axis=1), jnp.stack([theirs, mine], axis=1)
     )
     one_z = swap(one, Z, 2)
-    plan = make_plan(vert_blocks, one)
+    joined = one[0, 0, 0, :16]
+    plan = make_plan(vert_blocks, joined)
     tail = jnp.where(core == 1, keep[:, :ROWS], recv[:, :ROWS])
     tail = tail + one_z[0, 0, :, :1, :1] * 0
     prev = lax.ppermute(tail, "seq", [(i, i + 2) for i in range(126)])
-    own, foreign = split(queries, one)
+    own, foreign = split(queries, joined)
     other = swap(foreign, CORE, 1)
     near_own = band("band_own", False, plan, slash_offsets, own, keep, recv, prev)
     near_other = band("band_other", True, plan, slash_offsets, other, keep, recv, prev)

time: 78.7 us -> 76.8 us (0.976)
  waiting for transfers between devices: 12.8 us -> 11.7 us
    ppermute x15, waiting for transfers between devices: 7.99 us -> 6.66 us  [swap(): return lax.ppermute(block, 'seq', partner_route(axis, mask))]
  transfers between devices with their start and end apart: 17 -> 17, of which waited for: 8 -> 7; matrix products, arithmetic and copies ran while one was open for 2% -> 2% of each run, Pallas kernels for 42% -> 42%
where the time goes in v2:
time: 76.8 us; the launch traced here: 75.9 us
  Pallas kernels  39.8 us (52%)
  starting transfers between devices  21 us (27%)
  waiting for transfers between devices  11.7 us (15%)
  other arithmetic  2.29 us (3%)
  local copies, waits for them, and re-layouts  0.91 us (1%)
    pallas_call x4, Pallas kernels, vertical(): pl.pallas_call(functools.partial(vertical_kernel, groups, begin, len(piec...  27.7 us
    ppermute x15, starting transfers between devices, swap(): return lax.ppermute(block, 'seq', partner_route(axis, mask))  18.2 us
    ppermute x15, waiting for transfers between devices, swap(): return lax.ppermute(block, 'seq', partner_route(axis, mask))  6.66 us
    pallas_call x2, Pallas kernels, band(): pl.pallas_call(functools.partial(band_kernel, foreign), out_shape=STATE,...  4.52 us
    ppermute x1, waiting for transfers between devices, body(): prev = lax.ppermute(tail, 'seq', [(i, i + 2) for i in range(126)])  3.74 us
    pallas_call x1, Pallas kernels, make_plan(): pl.pallas_call(plan_kernel, out_shape=jax.ShapeDtypeStruct((9, 128), jnp....  3.23 us
    ppermute x1, starting transfers between devices, body(): prev = lax.ppermute(tail, 'seq', [(i, i + 2) for i in range(126)])  2.77 us
    pallas_call x1, Pallas kernels, split(): pl.pallas_call(split_kernel, out_shape=(shape, shape), in_specs=[vmem, vm...  2.21 us
  transfers between devices with their start and end apart: 17, of which 7 were waited for; matrix products, arithmetic and copies ran while one was open for 2% of the time, Pallas kernels for 42%

profile of v2, /device:TPU:31, one launch (start us, length us, event | category | flops | bytes accessed | tf_op | source)
XLA Modules:
  0.0 75.9 jit_solution(17926446413362544897)
XLA Ops:
  0.0 2.1 %prep.1 = (bf16[2,320,128]{2,1,0:T(8,128)(2,1)}, bf16[2,320,128]{2,1,0:T(8,128)(2,1)}, bf16[2,64,128]{2,1,0:T(8,128)(2,1)}, bf16[2,64,128]{2,1,0:T(8,128)(2,1)}) custom-call(s32[2,64]{1,0:T(2,128)} %vert_ref.3, bf16[256,256]{1,0:T(8,128)(2,1)} %keys_ref.1, bf16[256,256]{1,0:T(8,128)(2,1)} %values_ref.1), custom_call_target="tpu_custom_call" | custom-call | tf_op jit(solution)/shard_map/prep/pallas_call | solution.py:94
  2.1 0.7 collective-permute-start.1
  2.8 1.7 %collective-permute-start = (bf16[2,64,128]{2,1,0:T(8,128)(2,1)}, bf16[2,64,128]{2,1,0:T(8,128)(2,1)S(1)}, u32[]{:S(2)}, u32[]{:S(2)}) collective-permute-start(bf16[2,64,128]{2,1,0:T(8,128)(2,1)} %get-tuple-element.23), channel_id=1, source_target_pairs={{0,4},{2,6},{4,0},{6,2},{8,12},{10,14},{12,8},{14,10},{16,20},{18,... | collective-permute-start | bytes 98312 | tf_op jit(solution)/shard_map/ppermute | solution.py:43
  4.4 0.1 collective-permute-start.2
  4.5 1.4 %collective-permute-done = bf16[2,64,128]{2,1,0:T(8,128)(2,1)S(1)} collective-permute-done((bf16[2,64,128]{2,1,0:T(8,128)(2,1)}, bf16[2,64,128]{2,1,0:T(8,128)(2,1)S(1)}, u32[]{:S(2)}, u32[]{:S(2)}) %collective-permute-start) | collective-permute-done | bytes 32800 | tf_op jit(solution)/shard_map/ppermute | solution.py:43
  5.9 0.8 %maximum_bitcast_fusion = bf16[2,1,2,64,128]{4,3,2,0,1:T(8,128)(2,1)S(1)} fusion(bf16[1,2,64,128]{3,2,1,0:T(8,128)(2,1)S(1)} %bitcast.57, bf16[1,2,64,128]{3,2,1,0:T(8,128)(2,1)} %bitcast.55), kind=kLoop, calls=%fused_computation.12 | loop fusion | flops 32768 | bytes 131072 | tf_op jit(solution)/shard_map/stack | solution.py:420
  6.7 0.0 collective-permute-done.1.recv_ref
  6.7 1.3 %collective-permute-done.2 = bf16[2,64,128]{2,1,0:T(8,128)(2,1)S(1)} collective-permute-done((bf16[2,64,128]{2,1,0:T(8,128)(2,1)}, bf16[2,64,128]{2,1,0:T(8,128)(2,1)S(1)}, u32[]{:S(2)}, u32[]{:S(2)}) %collective-permute-start.2) | collective-permute-done | bytes 32800 | tf_op jit(solution)/shard_map/ppermute | solution.py:48
  8.0 0.6 slice_bitcast_fusion.1.after_ref
  8.6 3.0 %collective-permute-start.4 = (bf16[2,2,2,64,128]{4,3,2,0,1:T(8,128)(2,1)S(1)}, bf16[2,2,2,64,128]{4,3,2,0,1:T(8,128)(2,1)S(1)}, u32[]{:S(2)}, u32[]{:S(2)}) collective-permute-start(bf16[2,2,2,64,128]{4,3,2,0,1:T(8,128)(2,1)S(1)} %maximum_select_fusion.1), channel_id=1, source_target_pairs={{0,8},{2,10},{4,12},{6,14},{8,0},{10,2},{12,4},{14,6},{16,24},{18,... | collective-permute-start | bytes 393224 | tf_op jit(solution)/shard_map/ppermute | solution.py:43
  11.6 3.2 %plan.1.plan_ref.refs_0_ = s32[9,128]{1,0:T(8,128)} custom-call(s32[2,64]{1,0:T(2,128)} %vert_ref.3, bf16[16,128]{1,0:T(8,128)(2,1)} %slice_bitcast_fusion.1.after_ref), custom_call_target="tpu_custom_call" | custom-call | flops 3449999872 | bytes 4194304 | tf_op jit(solution)/shard_map/plan/pallas_call | solution.py:174
  14.9 0.0 copy-start
  14.9 2.2 %split.1 = (bf16[256,896]{1,0:T(8,128)(2,1)}, bf16[256,896]{1,0:T(8,128)(2,1)}) custom-call(bf16[256,1792]{1,0:T(8,128)(2,1)} %q_ref.1, bf16[16,128]{1,0:T(8,128)(2,1)} %slice_bitcast_fusion.1.after_ref), custom_call_target="tpu_custom_call" | custom-call | flops 1724999936 | bytes 4194304 | tf_op jit(solution)/shard_map/split/pallas_call | solution.py:163
  17.1 0.0 copy-start.1
  17.1 0.0 copy-start.2
  17.1 0.0 copy-start.3
  17.1 0.7 collective-permute-start.3
  17.8 0.4 collective-permute-done.4
  18.2 0.6 collective-permute-start.8
  18.9 0.5 collective-permute-start.6
  19.3 0.1 fusion.2
  19.4 0.0 copy-done
  19.4 0.1 fusion.1
  19.5 2.8 %collective-permute-start.5 = (bf16[2,256,128]{2,1,0:T(8,128)(2,1)S(1)}, bf16[2,256,128]{2,1,0:T(8,128)(2,1)S(1)}, u32[]{:S(2)}, u32[]{:S(2)}) collective-permute-start(bf16[2,256,128]{2,1,0:T(8,128)(2,1)S(1)} %fusion.1), channel_id=1, source_target_pairs={{0,4},{2,6},{4,8},{6,10},{8,12},{10,14},{12,16},{14,18},{16,20},{1... | collective-permute-start | bytes 393224 | tf_op jit(solution)/shard_map/ppermute | solution.py:427
  22.3 0.4 collective-permute-done.8
  22.7 0.6 collective-permute-start.9
  23.3 0.0 collective-permute-done.6
  23.3 0.9 %collective-permute-start.7 = (bf16[2,4,2,2,32,128]{5,4,3,1,2,0:T(8,128)(2,1)S(1)}, bf16[2,4,2,2,32,128]{5,4,3,1,2,0:T(8,128)(2,1)S(1)}, u32[]{:S(2)}, u32[]{:S(2)}) collective-permute-start(bf16[2,4,2,2,32,128]{5,4,3,1,2,0:T(8,128)(2,1)S(1)} %pad_maximum_fusion.2), channel_id=1, source_target_pairs={{0,48},{2,50},{4,52},{6,54},{8,56},{10,58},{12,60},{14,62},{16,32}... | collective-permute-start | bytes 786440 | tf_op jit(solution)/shard_map/ppermute | solution.py:43
  24.2 3.7 %collective-permute-done.5.prev_ref = bf16[2,256,128]{2,1,0:T(8,128)(2,1)S(1)} collective-permute-done((bf16[2,256,128]{2,1,0:T(8,128)(2,1)S(1)}, bf16[2,256,128]{2,1,0:T(8,128)(2,1)S(1)}, u32[]{:S(2)}, u32[]{:S(2)}) %collective-permute-start.5) | collective-permute-done | bytes 131104 | tf_op jit(solution)/shard_map/ppermute | solution.py:427
  27.9 0.0 copy-done.1
  27.9 0.0 copy-done.2
  27.9 0.0 copy-done.3
  27.9 2.3 %band_own.1 = (f32[7,256,256]{2,1,0:T(8,128)S(1)}, f32[7,256,128]{2,1,0:T(8,128)S(1)}) custom-call(s32[9,128]{1,0:T(8,128)S(1)} %copy-done.3, s32[2,3]{1,0:T(2,128)S(1)} %copy-done.1, bf16[256,896]{1,0:T(8,128)(2,1)S(1)} %copy-done.2, bf16[2,320,128]{2,1,0:T(8,128)(2,1)S(1)} %copy-done, bf16[2,320,128]{2,1,0:T(8,128)(2,1)S(1)} %collective-permute-done.1.recv_ref, ...), custom_call_target="tpu_custom_call" | custom-call | flops 3449999872 | bytes 4194304 | tf_op jit(solution)/shard_map/band_own/pallas_call | solution.py:242
  30.2 0.0 collective-permute-done.3.q_ref.refs_2_.refs_1_
  30.2 2.3 %band_other.1 = (f32[7,256,256]{2,1,0:T(8,128)S(1)}, f32[7,256,128]{2,1,0:T(8,128)S(1)}) custom-call(s32[9,128]{1,0:T(8,128)S(1)} %copy-done.3, s32[2,3]{1,0:T(2,128)S(1)} %copy-done.1, bf16[256,896]{1,0:T(8,128)(2,1)S(1)} %collective-permute-done.3.q_ref.refs_2_.refs_1_, bf16[2,320,128]{2,1,0:T(8,128)(2,1)S(1)} %copy-done, ...), custom_call_target="tpu_custom_call" | custom-call | flops 3449999872 | bytes 4194304 | tf_op jit(solution)/shard_map/band_other/pallas_call | solution.py:242
  32.5 0.0 collective-permute-done.7
  32.5 0.1 pad_maximum_fusion
  32.6 0.9 %collective-permute-start.12 = (bf16[4,4,2,2,32,128]{5,4,3,1,2,0:T(8,128)(2,1)S(1)}, bf16[4,4,2,2,32,128]{5,4,3,1,2,0:T(8,128)(2,1)S(1)}, u32[]{:S(2)}, u32[]{:S(2)}) collective-permute-start(bf16[4,4,2,2,32,128]{5,4,3,1,2,0:T(8,128)(2,1)S(1)} %pad_maximum_fusion), channel_id=1, source_target_pairs={{0,192},{2,194},{4,196},{6,198},{8,200},{10,202},{12,204},{14,206}... | collective-permute-start | bytes 1572872 | tf_op jit(solution)/shard_map/ppermute | solution.py:43
  33.6 0.5 collective-permute-start.10
  34.1 0.0 collective-permute-done.9
  34.1 0.1 pad_maximum_fusion.1
  34.2 3.5 %collective-permute-start.13 = (bf16[4,4,2,2,32,128]{5,4,3,1,2,0:T(8,128)(2,1)S(1)}, bf16[4,4,2,2,32,128]{5,4,3,1,2,0:T(8,128)(2,1)S(1)}, u32[]{:S(2)}, u32[]{:S(2)}) collective-permute-start(bf16[4,4,2,2,32,128]{5,4,3,1,2,0:T(8,128)(2,1)S(1)} %pad_maximum_fusion.1), channel_id=1, source_target_pairs={{0,48},{2,50},{4,52},{6,54},{8,56},{10,58},{12,60},{14,62},{16,32}... | collective-permute-start | bytes 1572872 | tf_op jit(solution)/shard_map/ppermute | solution.py:43
  37.7 0.0 collective-permute-start.11
  37.7 5.8 %near.1 = (f32[7,256,256]{2,1,0:T(8,128)S(1)}, f32[7,256,128]{2,1,0:T(8,128)S(1)}, f32[7,256,256]{2,1,0:T(8,128)S(1)}, f32[7,256,128]{2,1,0:T(8,128)S(1)}) custom-call(s32[9,128]{1,0:T(8,128)S(1)} %copy-done.3, bf16[256,896]{1,0:T(8,128)(2,1)S(1)} %copy-done.2, bf16[256,896]{1,0:T(8,128)(2,1)S(1)} %collective-permute-done.3.q_ref.refs_2_.refs_1_, ...), custom_call_target="tpu_custom_call" | custom-call | flops 6899999744 | bytes 4194304 | tf_op jit(solution)/shard_map/near/pallas_call | solution.py:392
  43.5 1.5 %collective-permute-done.12 = bf16[4,4,2,2,32,128]{5,4,3,1,2,0:T(8,128)(2,1)S(1)} collective-permute-done((bf16[4,4,2,2,32,128]{5,4,3,1,2,0:T(8,128)(2,1)S(1)}, bf16[4,4,2,2,32,128]{5,4,3,1,2,0:T(8,128)(2,1)S(1)}, u32[]{:S(2)}, u32[]{:S(2)}) %collective-permute-start.12) | collective-permute-done | bytes 524320 | tf_op jit(solution)/shard_map/ppermute | solution.py:43
  45.0 0.1 collective-permute-start.14
  45.1 3.0 %collective-permute-done.13 = bf16[4,4,2,2,32,128]{5,4,3,1,2,0:T(8,128)(2,1)S(1)} collective-permute-done((bf16[4,4,2,2,32,128]{5,4,3,1,2,0:T(8,128)(2,1)S(1)}, bf16[4,4,2,2,32,128]{5,4,3,1,2,0:T(8,128)(2,1)S(1)}, u32[]{:S(2)}, u32[]{:S(2)}) %collective-permute-start.13) | collective-permute-done | bytes 524320 | tf_op jit(solution)/shard_map/ppermute | solution.py:43
  48.1 1.6 %collective-permute-start.15 = (bf16[4,4,2,2,32,128]{5,4,3,1,2,0:T(8,128)(2,1)S(1)}, bf16[4,4,2,2,32,128]{5,4,3,1,2,0:T(8,128)(2,1)S(1)}, u32[]{:S(2)}, u32[]{:S(2)}) collective-permute-start(bf16[4,4,2,2,32,128]{5,4,3,1,2,0:T(8,128)(2,1)S(1)} %collective-permute-done.13), channel_id=1, source_target_pairs={{0,16},{2,18},{4,20},{6,22},{8,24},{10,26},{12,28},{14,30},{16,0},... | collective-permute-start | bytes 1572872 | tf_op jit(solution)/shard_map/ppermute | solution.py:43
  49.7 0.0 collective-permute-done.10
  49.7 0.0 collective-permute-done.11
  49.8 10.9 %middle.1 = (f32[7,256,256]{2,1,0:T(8,128)S(1)}, f32[7,256,128]{2,1,0:T(8,128)S(1)}, f32[7,256,256]{2,1,0:T(8,128)S(1)}, f32[7,256,128]{2,1,0:T(8,128)S(1)}) custom-call(s32[9,128]{1,0:T(8,128)S(1)} %copy-done.3, bf16[256,896]{1,0:T(8,128)(2,1)S(1)} %copy-done.2, bf16[256,896]{1,0:T(8,128)(2,1)S(1)} %collective-permute-done.3.q_ref.refs_2_.refs_1_, ...), custom_call_target="tpu_custom_call" | custom-call | flops 13799999488 | bytes 4194304 | tf_op jit(solution)/shard_map/middle/pallas_call | solution.py:392
  60.7 0.0 collective-permute-done.14
  60.7 0.0 collective-permute-done.15
  60.8 5.5 %far.1 = bf16[256,896]{1,0:T(8,128)(2,1)S(1)} custom-call(s32[9,128]{1,0:T(8,128)S(1)} %copy-done.3, bf16[256,896]{1,0:T(8,128)(2,1)S(1)} %collective-permute-done.3.q_ref.refs_2_.refs_1_, f32[7,256,256]{2,1,0:T(8,128)S(1)} %get-tuple-element.39.refs_2_, f32[7,256,128]{2,1,0:T(8,128)S(1)} %get-tuple-element.40.refs_3_, ...), custom_call_target="tpu_custom_call" | custom-call | flops 4600000000 | bytes 4194304 | tf_op jit(solution)/shard_map/far/pallas_call | solution.py:392
  66.3 3.0 %collective-permute-start.16 = (bf16[256,896]{1,0:T(8,128)(2,1)S(1)}, bf16[256,896]{1,0:T(8,128)(2,1)S(1)}, u32[]{:S(2)}, u32[]{:S(2)}) collective-permute-start(bf16[256,896]{1,0:T(8,128)(2,1)S(1)} %far.1), channel_id=1, source_target_pairs={{0,2},{2,0},{4,6},{6,4},{8,10},{10,8},{12,14},{14,12},{16,18},{18,... | collective-permute-start | bytes 1376264 | tf_op jit(solution)/shard_map/ppermute | solution.py:43
  69.3 5.5 %last.1 = bf16[256,896]{1,0:T(8,128)(2,1)S(1)} custom-call(s32[9,128]{1,0:T(8,128)S(1)} %copy-done.3, bf16[256,896]{1,0:T(8,128)(2,1)S(1)} %copy-done.2, f32[7,256,256]{2,1,0:T(8,128)S(1)} %get-tuple-element.37.refs_2_, f32[7,256,128]{2,1,0:T(8,128)S(1)} %get-tuple-element.38.refs_3_, bf16[32,2,32,128]{3,2,1,0:T(8,128)(2,1)S(1)} %bitcast.26, ...), custom_call_target="tpu_custom_call" | custom-call | flops 4600000000 | bytes 4194304 | tf_op jit(solution)/shard_map/last/pallas_call | solution.py:392
  74.8 0.0 collective-permute-done.16
  74.8 1.1 %maximum_select_fusion = bf16[256,1792]{1,0:T(8,128)(2,1)} fusion(bf16[256,896]{1,0:T(8,128)(2,1)S(1)} %collective-permute-done.16, bf16[256,896]{1,0:T(8,128)(2,1)S(1)} %last.1, pred[]{:T(512)S(6)} %eq.7), kind=kLoop, calls=%fused_computation | loop fusion | flops 4128768 | bytes 1835009 | tf_op jit(solution)/shard_map/jit(_where)/select_n | solution.py:449
  (14 shorter events, 0.4 us)
Async XLA Ops:
  2.1 4.6 %collective-permute-start.1 = (bf16[2,320,128]{2,1,0:T(8,128)(2,1)}, bf16[2,320,128]{2,1,0:T(8,128)(2,1)S(1)}, u32[]{:S(2)}, u32[]{:S(2)}) collective-permute-start(bf16[2,320,128]{2,1,0:T(8,128)(2,1)} %get-tuple-element.24), channel_id=1, source_target_pairs={{0,2},{2,0},{4,6},{6,4},{8,10},{10,8},{12,14},{14,12},{16,18},{18,... | collective-permute-start | bytes 491528 | tf_op jit(solution)/shard_map/ppermute | solution.py:43
  2.8 3.1 %collective-permute-start = (bf16[2,64,128]{2,1,0:T(8,128)(2,1)}, bf16[2,64,128]{2,1,0:T(8,128)(2,1)S(1)}, u32[]{:S(2)}, u32[]{:S(2)}) collective-permute-start(bf16[2,64,128]{2,1,0:T(8,128)(2,1)} %get-tuple-element.23), channel_id=1, source_target_pairs={{0,4},{2,6},{4,0},{6,2},{8,12},{10,14},{12,8},{14,10},{16,20},{18,... | collective-permute-start | bytes 98312 | tf_op jit(solution)/shard_map/ppermute | solution.py:43
  4.4 3.6 %collective-permute-start.2 = (bf16[2,64,128]{2,1,0:T(8,128)(2,1)}, bf16[2,64,128]{2,1,0:T(8,128)(2,1)S(1)}, u32[]{:S(2)}, u32[]{:S(2)}) collective-permute-start(bf16[2,64,128]{2,1,0:T(8,128)(2,1)} %get-tuple-element.25), channel_id=1, source_target_pairs={{0,6},{2,4},{4,2},{6,0},{8,14},{10,12},{12,10},{14,8},{16,22},{18,... | collective-permute-start | bytes 98312 | tf_op jit(solution)/shard_map/ppermute | solution.py:48
  8.6 9.6 %collective-permute-start.4 = (bf16[2,2,2,64,128]{4,3,2,0,1:T(8,128)(2,1)S(1)}, bf16[2,2,2,64,128]{4,3,2,0,1:T(8,128)(2,1)S(1)}, u32[]{:S(2)}, u32[]{:S(2)}) collective-permute-start(bf16[2,2,2,64,128]{4,3,2,0,1:T(8,128)(2,1)S(1)} %maximum_select_fusion.1), channel_id=1, source_target_pairs={{0,8},{2,10},{4,12},{6,14},{8,0},{10,2},{12,4},{14,6},{16,24},{18,... | collective-permute-start | bytes 393224 | tf_op jit(solution)/shard_map/ppermute | solution.py:43
  14.9 4.6 %copy-start = (bf16[2,320,128]{2,1,0:T(8,128)(2,1)S(1)}, bf16[2,320,128]{2,1,0:T(8,128)(2,1)}, u32[]{:S(2)}) copy-start(bf16[2,320,128]{2,1,0:T(8,128)(2,1)} %get-tuple-element.28.keep_ref) | copy-start | bytes 491524
  17.1 10.8 %copy-start.1 = (s32[2,3]{1,0:T(2,128)S(1)}, s32[2,3]{1,0:T(2,128)}, u32[]{:S(2)}) copy-start(s32[2,3]{1,0:T(2,128)} %slash_ref.3) | copy-start | bytes 76
  17.1 10.8 %copy-start.2 = (bf16[256,896]{1,0:T(8,128)(2,1)S(1)}, bf16[256,896]{1,0:T(8,128)(2,1)}, u32[]{:S(2)}) copy-start(bf16[256,896]{1,0:T(8,128)(2,1)} %get-tuple-element.26.q_ref.refs_1_) | copy-start | bytes 1376260
  17.1 10.8 %copy-start.3 = (s32[9,128]{1,0:T(8,128)S(1)}, s32[9,128]{1,0:T(8,128)}, u32[]{:S(2)}) copy-start(s32[9,128]{1,0:T(8,128)} %plan.1.plan_ref.refs_0_) | copy-start | bytes 13828
  17.1 13.1 %collective-permute-start.3 = (bf16[256,896]{1,0:T(8,128)(2,1)}, bf16[256,896]{1,0:T(8,128)(2,1)S(1)}, u32[]{:S(2)}, u32[]{:S(2)}) collective-permute-start(bf16[256,896]{1,0:T(8,128)(2,1)} %get-tuple-element.27), channel_id=1, source_target_pairs={{0,2},{2,0},{4,6},{6,4},{8,10},{10,8},{12,14},{14,12},{16,18},{18,... | collective-permute-start | bytes 1376264 | tf_op jit(solution)/shard_map/ppermute | solution.py:43
  18.2 4.4 %collective-permute-start.8 = (bf16[4,2,2,32,128]{4,3,2,0,1:T(8,128)(2,1)S(1)}, bf16[4,2,2,32,128]{4,3,2,0,1:T(8,128)(2,1)S(1)}, u32[]{:S(2)}, u32[]{:S(2)}) collective-permute-start(bf16[4,2,2,32,128]{4,3,2,0,1:T(8,128)(2,1)S(1)} %get-tuple-element.41), channel_id=1, source_target_pairs={{0,64},{2,66},{4,68},{6,70},{8,72},{10,74},{12,76},{14,78},{16,80}... | collective-permute-start | bytes 393224 | tf_op jit(solution)/shard_map/ppermute | solution.py:43
  18.9 4.4 %collective-permute-start.6 = (bf16[4,2,2,32,128]{4,3,2,0,1:T(8,128)(2,1)S(1)}, bf16[4,2,2,32,128]{4,3,2,0,1:T(8,128)(2,1)S(1)}, u32[]{:S(2)}, u32[]{:S(2)}) collective-permute-start(bf16[4,2,2,32,128]{4,3,2,0,1:T(8,128)(2,1)S(1)} %get-tuple-element.42), channel_id=1, source_target_pairs={{0,16},{2,18},{4,20},{6,22},{8,24},{10,26},{12,28},{14,30},{16,0},... | collective-permute-start | bytes 393224 | tf_op jit(solution)/shard_map/ppermute | solution.py:43
  19.5 8.4 %collective-permute-start.5 = (bf16[2,256,128]{2,1,0:T(8,128)(2,1)S(1)}, bf16[2,256,128]{2,1,0:T(8,128)(2,1)S(1)}, u32[]{:S(2)}, u32[]{:S(2)}) collective-permute-start(bf16[2,256,128]{2,1,0:T(8,128)(2,1)S(1)} %fusion.1), channel_id=1, source_target_pairs={{0,4},{2,6},{4,8},{6,10},{8,12},{10,14},{12,16},{14,18},{16,20},{1... | collective-permute-start | bytes 393224 | tf_op jit(solution)/shard_map/ppermute | solution.py:427
  22.7 11.4 %collective-permute-start.9 = (bf16[2,4,2,2,32,128]{5,4,3,1,2,0:T(8,128)(2,1)S(1)}, bf16[2,4,2,2,32,128]{5,4,3,1,2,0:T(8,128)(2,1)S(1)}, u32[]{:S(2)}, u32[]{:S(2)}) collective-permute-start(bf16[2,4,2,2,32,128]{5,4,3,1,2,0:T(8,128)(2,1)S(1)} %pad_maximum_fusion.3), channel_id=1, source_target_pairs={{0,192},{2,194},{4,196},{6,198},{8,200},{10,202},{12,204},{14,206}... | collective-permute-start | bytes 786440 | tf_op jit(solution)/shard_map/ppermute | solution.py:43
  23.3 9.2 %collective-permute-start.7 = (bf16[2,4,2,2,32,128]{5,4,3,1,2,0:T(8,128)(2,1)S(1)}, bf16[2,4,2,2,32,128]{5,4,3,1,2,0:T(8,128)(2,1)S(1)}, u32[]{:S(2)}, u32[]{:S(2)}) collective-permute-start(bf16[2,4,2,2,32,128]{5,4,3,1,2,0:T(8,128)(2,1)S(1)} %pad_maximum_fusion.2), channel_id=1, source_target_pairs={{0,48},{2,50},{4,52},{6,54},{8,56},{10,58},{12,60},{14,62},{16,32}... | collective-permute-start | bytes 786440 | tf_op jit(solution)/shard_map/ppermute | solution.py:43
  32.6 12.3 %collective-permute-start.12 = (bf16[4,4,2,2,32,128]{5,4,3,1,2,0:T(8,128)(2,1)S(1)}, bf16[4,4,2,2,32,128]{5,4,3,1,2,0:T(8,128)(2,1)S(1)}, u32[]{:S(2)}, u32[]{:S(2)}) collective-permute-start(bf16[4,4,2,2,32,128]{5,4,3,1,2,0:T(8,128)(2,1)S(1)} %pad_maximum_fusion), channel_id=1, source_target_pairs={{0,192},{2,194},{4,196},{6,198},{8,200},{10,202},{12,204},{14,206}... | collective-permute-start | bytes 1572872 | tf_op jit(solution)/shard_map/ppermute | solution.py:43
  33.6 16.1 %collective-permute-start.10 = (bf16[4,4,2,2,32,128]{5,4,3,1,2,0:T(8,128)(2,1)S(1)}, bf16[4,4,2,2,32,128]{5,4,3,1,2,0:T(8,128)(2,1)S(1)}, u32[]{:S(2)}, u32[]{:S(2)}) collective-permute-start(bf16[4,4,2,2,32,128]{5,4,3,1,2,0:T(8,128)(2,1)S(1)} %pad_maximum_fusion), channel_id=1, source_target_pairs={{0,64},{2,66},{4,68},{6,70},{8,72},{10,74},{12,76},{14,78},{16,80}... | collective-permute-start | bytes 1572872 | tf_op jit(solution)/shard_map/ppermute | solution.py:43
  34.2 13.9 %collective-permute-start.13 = (bf16[4,4,2,2,32,128]{5,4,3,1,2,0:T(8,128)(2,1)S(1)}, bf16[4,4,2,2,32,128]{5,4,3,1,2,0:T(8,128)(2,1)S(1)}, u32[]{:S(2)}, u32[]{:S(2)}) collective-permute-start(bf16[4,4,2,2,32,128]{5,4,3,1,2,0:T(8,128)(2,1)S(1)} %pad_maximum_fusion.1), channel_id=1, source_target_pairs={{0,48},{2,50},{4,52},{6,54},{8,56},{10,58},{12,60},{14,62},{16,32}... | collective-permute-start | bytes 1572872 | tf_op jit(solution)/shard_map/ppermute | solution.py:43
  37.7 12.0 %collective-permute-start.11 = (bf16[4,4,2,2,32,128]{5,4,3,1,2,0:T(8,128)(2,1)S(1)}, bf16[4,4,2,2,32,128]{5,4,3,1,2,0:T(8,128)(2,1)S(1)}, u32[]{:S(2)}, u32[]{:S(2)}) collective-permute-start(bf16[4,4,2,2,32,128]{5,4,3,1,2,0:T(8,128)(2,1)S(1)} %pad_maximum_fusion.1), channel_id=1, source_target_pairs={{0,16},{2,18},{4,20},{6,22},{8,24},{10,26},{12,28},{14,30},{16,0},... | collective-permute-start | bytes 1572872 | tf_op jit(solution)/shard_map/ppermute | solution.py:43
  45.0 15.7 %collective-permute-start.14 = (bf16[4,4,2,2,32,128]{5,4,3,1,2,0:T(8,128)(2,1)S(1)}, bf16[4,4,2,2,32,128]{5,4,3,1,2,0:T(8,128)(2,1)S(1)}, u32[]{:S(2)}, u32[]{:S(2)}) collective-permute-start(bf16[4,4,2,2,32,128]{5,4,3,1,2,0:T(8,128)(2,1)S(1)} %collective-permute-done.12), channel_id=1, source_target_pairs={{0,64},{2,66},{4,68},{6,70},{8,72},{10,74},{12,76},{14,78},{16,80}... | collective-permute-start | bytes 1572872 | tf_op jit(solution)/shard_map/ppermute | solution.py:43
  48.1 12.6 %collective-permute-start.15 = (bf16[4,4,2,2,32,128]{5,4,3,1,2,0:T(8,128)(2,1)S(1)}, bf16[4,4,2,2,32,128]{5,4,3,1,2,0:T(8,128)(2,1)S(1)}, u32[]{:S(2)}, u32[]{:S(2)}) collective-permute-start(bf16[4,4,2,2,32,128]{5,4,3,1,2,0:T(8,128)(2,1)S(1)} %collective-permute-done.13), channel_id=1, source_target_pairs={{0,16},{2,18},{4,20},{6,22},{8,24},{10,26},{12,28},{14,30},{16,0},... | collective-permute-start | bytes 1572872 | tf_op jit(solution)/shard_map/ppermute | solution.py:43
  66.3 8.5 %collective-permute-start.16 = (bf16[256,896]{1,0:T(8,128)(2,1)S(1)}, bf16[256,896]{1,0:T(8,128)(2,1)S(1)}, u32[]{:S(2)}, u32[]{:S(2)}) collective-permute-start(bf16[256,896]{1,0:T(8,128)(2,1)S(1)} %far.1), channel_id=1, source_target_pairs={{0,2},{2,0},{4,6},{6,4},{8,10},{10,8},{12,14},{14,12},{16,18},{18,... | collective-permute-start | bytes 1376264 | tf_op jit(solution)/shard_map/ppermute | solution.py:43
